TPU v7x, 256 devices: a whole 4x4x8 slice. The times are simulated.
256 devices in a mesh: expert: 8 (over x, core), fsdp: 32 (over z, y).
Axes of the slice: x: 4, y: 4, z: 8, core: 2. Of those that a mesh axis runs over, the one named last changes fastest.
Arguments:
- weights: bfloat16 [8, 8192, 4608], P('expert', 'fsdp'), may hold values from -0.09375 to 0.09375
- gaussian: bfloat16 [8192, 640], P('fsdp'), may hold values from -6 to 6
Outputs:
- orthonormal: float32 [8, 4608, 640], P('expert', 'fsdp')
- projection: float32 [8, 8192, 640], P('expert', 'fsdp')
All inputs are finite; a program needn't handle non-finite values.
Results may differ from a plain program's by a relative error of at most 0.015.
Values may be sent and summed in bfloat16 or wider, within the bound.
A program may use at most 128 MiB of HBM per device.

v0:
```python
import jax
import jax.numpy as jnp
from jax import lax
from jax.sharding import PartitionSpec as P

D = 4608


def factor_basis(sketch_part, gram_matrix):
    lower_factor = jnp.linalg.cholesky(gram_matrix)
    return jax.scipy.linalg.solve_triangular(lower_factor, sketch_part.T, lower=True).T


def on_device(weights, gaussian):
    summed = lax.psum(weights.astype(jnp.float32).astype(jnp.bfloat16), "expert").astype(
        jnp.float32
    )
    mean_weight = summed / lax.axis_size("expert")
    deltas = (weights[0].astype(jnp.float32) - mean_weight[0]).astype(jnp.bfloat16)
    columns = deltas
    sketch = lax.psum_scatter(
        lax.dot_general(
            columns, gaussian, (((0,), (0,)), ((), ())), preferred_element_type=jnp.float32
        ),
        "fsdp",
        scatter_dimension=0,
        tiled=True,
    )
    partial_gram = jnp.dot(sketch.T, sketch, precision=lax.Precision.HIGHEST)
    gram_matrix = lax.psum(partial_gram, "fsdp") / D
    orthonormal = factor_basis(sketch, gram_matrix)
    basis_copy = orthonormal.astype(jnp.bfloat16)
    columns = deltas
    projection = jnp.dot(
        columns,
        lax.all_gather(basis_copy, "fsdp", axis=0, tiled=True),
        preferred_element_type=jnp.float32,
    )
    return (orthonormal[None], projection[None])


def solution(mesh):
    in_specs = (P("expert", "fsdp", None), P("fsdp", None))
    out_specs = (P("expert", "fsdp", None), P("expert", "fsdp", None))
    return jax.shard_map(
        on_device, mesh=mesh, in_specs=in_specs, out_specs=out_specs, check_vma=False
    )
```

profile of v0, /device:TPU:8, one launch (start us, length us, event | category | flops | bytes accessed | tf_op | source)
XLA Modules:
  0.0 776.1 jit_solution(11174023627219361579)
XLA Ops:
  7.2 0.7 all-reduce.4.cloned.1.call-update
  8.0 77.0 %all-reduce.4.cloned.1.call-done = bf16[1,256,4608]{2,1,0:T(8,128)(2,1)} async-done(((bf16[1,256,4608]{2,1,0:T(8,128)(2,1)}), bf16[1,256,4608]{2,1,0:T(8,128)(2,1)}) %all-reduce.4.cloned.1.call-update) | async-done | bytes 2359312 | tf_op jit(solution)/shard_map/psum | solution.py:15
  84.9 8.2 %fusion.3 = f32[4608,640]{1,0:T(8,128)} fusion(bf16[256,640]{1,0:T(8,128)(2,1)S(1)} %copy-done, bf16[1,256,4608]{2,1,0:T(8,128)(2,1)} %all-reduce.4.cloned.1.call-done, bf16[1,256,4608]{2,1,0:T(8,128)(2,1)S(1)} %copy-done.1), kind=kOutput, calls=%fused_computation.22 | convolution fusion | flops 1515847680 | bytes 16842752 | tf_op jit(solution)/shard_map/dot_general | solution.py:22
  93.2 236.3 %reduce-scatter.2.cloned.1.call-done = f32[144,640]{1,0:T(8,128)} async-done(((f32[4608,640]{1,0:T(8,128)}), f32[144,640]{1,0:T(8,128)}) %reduce-scatter.2.cloned.1.call-update) | async-done | bytes 368656 | tf_op jit(solution)/shard_map/reduce_scatter | solution.py:21
  329.5 4.1 fusion.50
  333.7 149.7 %all-reduce.6.cloned.1.call-done = f32[640,640]{0,1:T(8,128)} async-done(((f32[640,640]{0,1:T(8,128)}), f32[640,640]{0,1:T(8,128)}) %all-reduce.6.cloned.1.call-update) | async-done | bytes 1638416 | tf_op jit(solution)/shard_map/psum | solution.py:30
  483.4 2.7 broadcast_multiply_fusion
  486.1 3.4 copy.5
  489.5 1.6 fusion.1
  491.1 1.2 copy-done.4
  492.3 11.7 %cholesky.133 = f32[128,128]{1,0:T(8,128)S(1)} custom-call(f32[128,128]{1,0:T(8,128)S(1)} %cholesky.340), custom_call_target="Cholesky" | custom-call | tf_op jit(solution)/shard_map/jit(cholesky)/cholesky | solution.py:10
  504.1 9.8 %custom-call.39 = f32[1,128,128]{1,2,0:T(8,128)S(1)} custom-call(f32[1,128,128]{2,1,0:T(8,128)S(1)} %get-tuple-element.32), custom_call_target="InvertDiagBlocksLowerTriangular" | custom-call | tf_op jit(solution)/shard_map/jit(cholesky)/cholesky | solution.py:10
  514.0 1.3 constant_dynamic-update-slice_fusion.8
  515.3 1.3 convolution_subtract_fusion
  516.7 11.7 %cholesky.272 = f32[128,128]{1,0:T(8,128)S(1)} custom-call(f32[128,128]{1,0:T(8,128)S(1)} %cholesky.344), custom_call_target="Cholesky" | custom-call | tf_op jit(solution)/shard_map/jit(cholesky)/cholesky | solution.py:10
  528.4 10.0 %custom-call.40 = f32[1,128,128]{1,2,0:T(8,128)S(1)} custom-call(f32[1,128,128]{2,1,0:T(8,128)S(1)} %get-tuple-element.29), custom_call_target="InvertDiagBlocksLowerTriangular" | custom-call | tf_op jit(solution)/shard_map/jit(cholesky)/cholesky | solution.py:10
  538.7 1.4 convolution_subtract_fusion.1
  540.1 11.7 %cholesky.293 = f32[128,128]{1,0:T(8,128)S(1)} custom-call(f32[128,128]{1,0:T(8,128)S(1)} %cholesky.349), custom_call_target="Cholesky" | custom-call | tf_op jit(solution)/shard_map/jit(cholesky)/cholesky | solution.py:10
  551.9 0.6 compare_reduce_fusion.2
  552.5 9.8 %custom-call.41 = f32[1,128,128]{1,2,0:T(8,128)S(1)} custom-call(f32[1,128,128]{2,1,0:T(8,128)S(1)} %get-tuple-element.26), custom_call_target="InvertDiagBlocksLowerTriangular" | custom-call | tf_op jit(solution)/shard_map/jit(cholesky)/cholesky | solution.py:10
  562.6 1.4 convolution_subtract_fusion.2
  564.0 11.9 %cholesky.312 = f32[128,128]{1,0:T(8,128)S(1)} custom-call(f32[128,128]{1,0:T(8,128)S(1)} %cholesky.354), custom_call_target="Cholesky" | custom-call | tf_op jit(solution)/shard_map/jit(cholesky)/cholesky | solution.py:10
  575.9 0.7 compare_reduce_fusion.1
  576.6 9.8 %custom-call.42 = f32[1,128,128]{1,2,0:T(8,128)S(1)} custom-call(f32[1,128,128]{2,1,0:T(8,128)S(1)} %get-tuple-element.23), custom_call_target="InvertDiagBlocksLowerTriangular" | custom-call | tf_op jit(solution)/shard_map/jit(cholesky)/cholesky | solution.py:10
  586.6 1.2 convolution_subtract_fusion.7
  587.9 11.7 %cholesky.329 = f32[128,128]{1,0:T(8,128)S(1)} custom-call(f32[128,128]{1,0:T(8,128)S(1)} %convolution_subtract_fusion.7), custom_call_target="Cholesky" | custom-call | tf_op jit(solution)/shard_map/jit(cholesky)/cholesky | solution.py:10
  599.6 0.7 compare_reduce_fusion
  600.3 0.6 compare_reduce_fusion.3
  604.1 1.3 select_select_fusion
  605.4 14.0 %while.1 = (s32[]{:T(128)}, f32[640,640]{1,0:T(8,128)}, s32[5,2]{0,1:T(2,128)S(1)}, f32[5,128,128]{2,1,0:T(8,128)S(1)}, s32[]{:T(128)}) while((s32[]{:T(128)}, f32[640,640]{1,0:T(8,128)}, s32[5,2]{0,1:T(2,128)S(1)}, f32[5,128,128]{2,1,0:T(8,128)S(1)}, s32[]{:T(128)}) %tuple.37), condition=%wide.while_cond, body=%wide.while_body.sunk | while | flops 2 | bytes 131181 | solution.py:11
  606.0 2.2 bitcast_dynamic-update-slice_fusion.2
  608.3 0.5 fusion.62
  608.8 2.2 bitcast_dynamic-update-slice_fusion.2
  611.1 0.5 fusion.62
  611.6 2.2 bitcast_dynamic-update-slice_fusion.2
  614.5 2.2 bitcast_dynamic-update-slice_fusion.2
  617.3 2.1 bitcast_dynamic-update-slice_fusion.2
  619.4 49.4 %custom-call.43 = f32[5,128,128]{1,2,0:T(8,128)S(1)} custom-call(f32[5,128,128]{2,1,0:T(8,128)S(1)} %get-tuple-element.9), custom_call_target="InvertDiagBlocksLowerTriangular" | custom-call | tf_op jit(solution)/shard_map/jit(_solve_triangular)/triangular_solve | solution.py:11
  669.0 1.1 convolution_subtract_fusion.4
  670.4 1.3 convolution_subtract_fusion.3
  671.7 1.1 constant_dynamic-update-slice_fusion.1
  672.8 1.3 convolution_subtract_fusion.6
  674.1 1.1 constant_dynamic-update-slice_fusion
  675.2 1.4 convolution_subtract_fusion.5
  676.5 1.1 convolution_dynamic-update-slice_fusion.2
  677.6 0.7 bitcast_convert_fusion
  678.4 84.7 %all-gather.2.cloned.1.call-done = bf16[4608,640]{1,0:T(8,128)(2,1)} async-done(((bf16[144,640]{1,0:T(8,128)(2,1)}), bf16[4608,640]{1,0:T(8,128)(2,1)}) %all-gather.2.cloned.1.call-update) | async-done | bytes 5898256 | tf_op jit(solution)/shard_map/all_gather | solution.py:36
  763.1 6.2 convolution_bitcast_fusion
  (48 shorter events, 3.7 us)
Async XLA Ops:
  7.2 77.8 %copy-start = (bf16[256,640]{1,0:T(8,128)(2,1)S(1)}, bf16[256,640]{1,0:T(8,128)(2,1)}, u32[]{:S(2)}) copy-start(bf16[256,640]{1,0:T(8,128)(2,1)} %param.3) | copy-start | bytes 983044
  7.2 77.8 %copy-start.1 = (bf16[1,256,4608]{2,1,0:T(8,128)(2,1)S(1)}, bf16[1,256,4608]{2,1,0:T(8,128)(2,1)}, u32[]{:S(2)}) copy-start(bf16[1,256,4608]{2,1,0:T(8,128)(2,1)} %param.2) | copy-start | bytes 7077892
  7.2 77.8 %all-reduce.4.cloned.1.call-start = ((), (), s32[]{:S(2)}) async-start(), calls=%async_computation.1 | async-start | bytes 4718592 | tf_op jit(solution)/shard_map/psum | solution.py:15
  7.9 321.6 %reduce-scatter.2.cloned.1.call-start = ((), (), s32[]{:S(2)}) async-start(), calls=%async_computation.2 | async-start | bytes 12165120 | tf_op jit(solution)/shard_map/reduce_scatter | solution.py:21
  93.2 390.2 %all-reduce.6.cloned.1.call-start = ((), (), s32[]{:S(2)}) async-start(), calls=%async_computation.3 | async-start | bytes 3276800 | tf_op jit(solution)/shard_map/psum | solution.py:30
  333.6 429.5 %all-gather.2.cloned.1.call-start = ((), (), s32[]{:S(2)}) async-start(), calls=%async_computation.4 | async-start | bytes 6082560 | tf_op jit(solution)/shard_map/all_gather | solution.py:36
  486.1 3.4 copy-start.3
  491.1 1.2 copy-start.4
  604.1 64.7 %copy-start.5 = (f32[144,640]{1,0:T(8,128)S(1)}, f32[144,640]{1,0:T(8,128)}, u32[]{:S(2)}) copy-start(f32[144,640]{1,0:T(8,128)} %reduce-scatter.2.cloned.1.call-done) | copy-start | bytes 1105924
  668.8 1.4 copy-start.7
  670.4 92.7 %copy-start.2 = (bf16[1,256,4608]{2,1,0:T(8,128)(2,1)S(1)}, bf16[1,256,4608]{2,1,0:T(8,128)(2,1)}, u32[]{:S(2)}) copy-start(bf16[1,256,4608]{2,1,0:T(8,128)(2,1)} %param.2) | copy-start | bytes 7077892
  677.6 91.7 %copy-start.6 = (f32[640,144]{0,1:T(8,128)}, f32[640,144]{0,1:T(8,128)S(1)}, u32[]{:S(2)}) copy-start(f32[640,144]{0,1:T(8,128)S(1)} %convolution_dynamic-update-slice_fusion.2) | copy-start | bytes 1105924
Sparse Core Ops, SparseCore 0:
  10.4 74.4 all-reduce.3
  93.3 236.1 reduce-scatter.1
  333.7 149.5 all-reduce.5
  678.5 84.5 all-gather.1
where the time goes:
time: 782 us; the launch traced here: 776 us
  waiting for transfers between devices  548 us (70%)
  other arithmetic  157 us (20%)
  matrix products  34.6 us (4%)
  local copies, waits for them, and re-layouts  18.6 us (2%)
  between operations  17.5 us (2%)
    reduce_scatter x1, waiting for transfers between devices, on_device(): lax.psum_scatter(lax.dot_general(columns, gaussian, (((0,), (0,)), ((), (...  236 us
    psum x1, waiting for transfers between devices, on_device(): gram_matrix = lax.psum(partial_gram, 'fsdp') / D  150 us
    another operation x18, other arithmetic, factor_basis(): lower_factor = jnp.linalg.cholesky(gram_matrix)  101 us
    all_gather x1, waiting for transfers between devices, on_device(): lax.all_gather(basis_copy, 'fsdp', axis=0, tiled=True)  84.7 us
    psum x1, waiting for transfers between devices, on_device(): lax.psum(weights.astype(jnp.float32).astype(jnp.bfloat16), 'expert')  77 us
    another operation x3, other arithmetic, factor_basis(): jax.scipy.linalg.solve_triangular(lower_factor, sketch_part.T, lower=True)  50.7 us
  transfers between devices with their start and end apart: 4, of which 4 were waited for; matrix products, arithmetic and copies ran while one was open for 0% of the time, Pallas kernels for 0%

commit v1 on v0

v1 whole, which is shorter than its diff:
```python
import functools
import jax
import jax.numpy as jnp
from jax import lax
from jax.sharding import PartitionSpec as P
from jax.experimental import pallas as pl
from jax.experimental.pallas import tpu as pltpu

MESH = pl.DeviceIdType.MESH
NY, NZ = 4, 8
NB = 128

def rc(src, dst, ss, rs, dev):
    return pltpu.make_async_remote_copy(src_ref=src, dst_ref=dst, send_sem=ss, recv_sem=rs, device_id=dev,
                                        device_id_type=MESH)

def sketch_body(w_ref, g_ref, s_ref, wz_ref, wv, gv, p_ref, sbuf, rbuf, ysend, yrecv, gsend, grecv, fsend, frecv,
           zsend, zrecv, loc, *, SUBS):
    rows, D = w_ref.shape
    K = g_ref.shape[1]
    cw = D // NY
    ch = cw // NZ
    e = lax.axis_index("expert")
    f = lax.axis_index("fsdp")
    y = lax.rem(f, NY)
    z = f // NY
    core = lax.rem(e, 2)
    sib = (e + 1 - 2 * core, f)
    ydev = lambda d: (e, z * NY + lax.rem(y + d, NY))
    zdev = lambda d: (e, lax.rem(z + d + NZ, NZ) * NY + y)
    barrier = pltpu.get_barrier_semaphore()
    partners = [ydev(1), ydev(2), ydev(3), sib, zdev(1), zdev(-1)]
    for p in partners:
        pl.semaphore_signal(barrier, inc=1, device_id=p, device_id_type=MESH)
    pl.semaphore_wait(barrier, len(partners))

    hr = rows // 2
    myrow = pl.multiple_of(y * rows, rows)
    ghalf = pl.multiple_of(core * hr, hr)
    gcs = []
    for d in (1, 3, 2):
        c = rc(g_ref.at[pl.ds(ghalf, hr), :], gv.at[pl.ds(pl.multiple_of(y * rows + ghalf, hr), hr), :],
               gsend.at[d], grecv.at[d], ydev(d))
        c.start(); gcs.append((d, c))
    wcs = []
    for d in (1, 3, 2):
        yy = lax.rem(y + d, NY)
        c = rc(w_ref.at[:, pl.ds(pl.multiple_of(yy * cw, NB), cw)], wv.at[pl.ds(myrow, rows), :],
               ysend.at[d], yrecv.at[d], ydev(d))
        c.start(); wcs.append((d, c))
    lw = pltpu.make_async_copy(w_ref.at[:, pl.ds(pl.multiple_of(y * cw, NB), cw)], wv.at[pl.ds(myrow, rows), :], loc.at[0])
    lw.start()
    lg = pltpu.make_async_copy(g_ref, gv.at[pl.ds(myrow, rows), :], loc.at[1])
    lg.start()
    fcs = []
    for d, c in gcs:
        c.wait_recv()
        src = lax.rem(y - d + NY, NY)
        piece = pl.ds(pl.multiple_of(src * rows + ghalf, hr), hr)
        h = rc(gv.at[piece, :], gv.at[piece, :], fsend.at[d], frecv.at[d], sib)
        h.start(); fcs.append(h)
    lw.wait(); lg.wait()
    for h in fcs:
        h.wait_recv()
    for d, c in wcs:
        c.wait_recv()
    out = pltpu.make_async_copy(wv, wz_ref, loc.at[2])
    out.start()

    def block(i, _):
        o = pl.multiple_of(i * NB, NB)
        p_ref[pl.ds(o, NB), :] = lax.dot_general(wv[:, pl.ds(o, NB)], gv[...], (((0,), (0,)), ((), ())),
                                                 preferred_element_type=jnp.float32)
        return 0
    lax.fori_loop(0, cw // NB, block, 0)

    ha = 80
    prev = {}
    def own(t, r, n, c0, c1):
        return p_ref[pl.ds(pl.multiple_of(t * ch + r, 16), n), c0:c1]
    for s in range(4):
        for dr, sgn in ((0, 1), (1, -1)):
            t = lax.rem(z + sgn * (4 - s) + NZ, NZ)
            for u, (c0, c1) in enumerate(SUBS):
                if s == 0:
                    r, n = (0, ha) if dr == 0 else (ha, ch - ha)
                    sbuf[dr, s, r:r + n, c0:c1] = own(t, r, n, c0, c1).astype(jnp.bfloat16)
                else:
                    prev[dr, u].wait_recv()
                    if s == 1:
                        r, n = (0, ha) if dr == 0 else (ha, ch - ha)
                        q, m = (ha, ch - ha) if dr == 0 else (0, ha)
                        sbuf[dr, s, r:r + n, c0:c1] = (own(t, r, n, c0, c1) + rbuf[dr, 0, r:r + n, c0:c1].astype(jnp.float32)).astype(jnp.bfloat16)
                        sbuf[dr, s, q:q + m, c0:c1] = own(t, q, m, c0, c1).astype(jnp.bfloat16)
                    else:
                        sbuf[dr, s, :, c0:c1] = (own(t, 0, ch, c0, c1) + rbuf[dr, s - 1, :, c0:c1].astype(jnp.float32)).astype(jnp.bfloat16)
                    prev[dr, u].wait_send()
                    r, n = 0, ch
                c = rc(sbuf.at[dr, s, pl.ds(r, n), pl.ds(c0, c1 - c0)], rbuf.at[dr, s, pl.ds(r, n), pl.ds(c0, c1 - c0)],
                       zsend.at[dr, s, u], zrecv.at[dr, s, u], zdev(sgn))
                c.start()
                prev[dr, u] = c
    for u, (c0, c1) in enumerate(SUBS):
        prev[0, u].wait()
        prev[1, u].wait()
        s_ref[:, c0:c1] = (own(z, 0, ch, c0, c1) + rbuf[0, 3, :, c0:c1].astype(jnp.float32)
                           + rbuf[1, 3, :, c0:c1].astype(jnp.float32))
    for d, c in gcs:
        c.wait_send()
    for d, c in wcs:
        c.wait_send()
    for h in fcs:
        h.wait_send()
    out.wait()

def sketch_kernel(w, g, subs=((0, 384), (384, 640))):
    rows, D = w.shape; K = g.shape[1]
    cw = D // NY; ch = cw // NZ
    nu = len(subs)
    V = pl.BlockSpec(memory_space=pltpu.VMEM); A = pl.BlockSpec(memory_space=pl.ANY)
    DM = pltpu.SemaphoreType.DMA
    return pl.pallas_call(
        functools.partial(sketch_body, SUBS=subs),
        out_shape=(jax.ShapeDtypeStruct((ch, K), jnp.float32), jax.ShapeDtypeStruct((rows * NY, cw), jnp.bfloat16)),
        in_specs=[A, A], out_specs=(V, A),
        scratch_shapes=[pltpu.VMEM((rows * NY, cw), jnp.bfloat16), pltpu.VMEM((rows * NY, K), jnp.bfloat16),
                        pltpu.VMEM((cw, K), jnp.float32),
                        pltpu.VMEM((2, 4, ch, K), jnp.bfloat16), pltpu.VMEM((2, 4, ch, K), jnp.bfloat16),
                        DM((4,)), DM((4,)), DM((4,)), DM((4,)), DM((4,)), DM((4,)),
                        DM((2, 4, nu)), DM((2, 4, nu)), DM((3,))],
        compiler_params=pltpu.CompilerParams(collective_id=0, has_side_effects=True, vmem_limit_bytes=48 * 2**20),
        name="sketch_exchange",
    )(w, g)


HI = lax.Precision.HIGHEST


def base_inverse(t_ref, n_ref):
    sub = lax.broadcasted_iota(jnp.int32, (8, NB), 0)
    row = lax.broadcasted_iota(jnp.int32, (NB, NB), 0)
    col = lax.broadcasted_iota(jnp.int32, (NB, NB), 1)
    n_ref[...] = jnp.where(row == col, 1.0, 0.0).astype(jnp.float32)
    nsub = NB // 8
    cur_t, cur_n = t_ref[0:8, :], n_ref[0:8, :]
    for b in range(nsub):
        r0 = 8 * b
        last = b == nsub - 1
        c = [jnp.broadcast_to(cur_t[:, r0 + i:r0 + i + 1], (8, NB)) for i in range(8)]
        if not last:
            nt, nn = t_ref[r0 + 8:r0 + 16, :], n_ref[r0 + 8:r0 + 16, :]
            d = [jnp.broadcast_to(nt[:, r0 + i:r0 + i + 1], (8, NB)) for i in range(8)]
        for i in range(8):
            rs = lax.rsqrt(jnp.broadcast_to(c[i][i:i + 1, :], (8, NB)))
            m = c[i] * rs
            mk = {}
            for k in range(i + 1, 8):
                mk[k] = jnp.broadcast_to(m[k:k + 1, :], (8, NB))
                c[k] = c[k] - m * mk[k]
            mm = jnp.where(sub > i, m, 0.0)
            ft = jnp.broadcast_to(cur_t[i:i + 1, :], (8, NB)) * rs
            fn = jnp.broadcast_to(cur_n[i:i + 1, :], (8, NB)) * rs
            cur_t = jnp.where(sub == i, ft, cur_t - mm * ft)
            cur_n = jnp.where(sub == i, fn, cur_n - mm * fn)
            if not last:
                md = d[i] * rs
                for k in range(i + 1, 8):
                    d[k] = d[k] - md * mk[k]
                nt = nt - md * ft
                nn = nn - md * fn
        n_ref[r0:r0 + 8, :] = cur_n
        if not last:
            if b < nsub - 2:
                lt = cur_t[:, :]
                both = jnp.concatenate([cur_t, cur_n], axis=1)
                upd = lax.dot_general(lt, both, (((0,), (0,)), ((), ())), precision=HI,
                                      preferred_element_type=jnp.float32)
                t_ref[r0 + 16:, :] = t_ref[r0 + 16:, :] - upd[r0 + 16:, :NB]
                n_ref[r0 + 16:, :] = n_ref[r0 + 16:, :] - upd[r0 + 16:, NB:]
            cur_t, cur_n = nt, nn

def basis_body(gram_ref, s_ref, o_ref, ob_ref, x_ref, t_ref, n_ref, *, K, D):
    R = s_ref.shape[0]
    x_ref[0:K, :] = gram_ref[...] * (1.0 / D)
    x_ref[K:K + R, :] = s_ref[...]
    def step(j, _):
        off = pl.multiple_of(j * NB, NB)
        t_ref[...] = x_ref[pl.ds(off, NB), pl.ds(off, NB)]
        base_inverse(t_ref, n_ref)
        p = lax.dot_general(x_ref[:, pl.ds(off, NB)], n_ref[...], (((1,), (1,)), ((), ())), precision=HI,
                            preferred_element_type=jnp.float32)
        x_ref[K:K + R, pl.ds(off, NB)] = p[K:K + R]
        r = lax.broadcasted_iota(jnp.int32, (K, NB), 0)
        lk = jnp.where(r >= off + NB, p[0:K], 0.0)
        @pl.when(j < K // NB - 1)
        def _():
            x_ref[...] = x_ref[...] - lax.dot_general(p, lk, (((1,), (1,)), ((), ())), precision=HI,
                                                      preferred_element_type=jnp.float32)
        return 0
    lax.fori_loop(0, K // NB, step, 0)
    o_ref[...] = x_ref[K:K + R, :]
    ob_ref[...] = x_ref[K:K + R, :].astype(jnp.bfloat16)

def chol_basis(gram, s, D):
    K = gram.shape[0]; R = s.shape[0]
    return pl.pallas_call(
        functools.partial(basis_body, K=K, D=D),
        out_shape=(jax.ShapeDtypeStruct((R, K), jnp.float32), jax.ShapeDtypeStruct((R, K), jnp.bfloat16)),
        in_specs=[pl.BlockSpec(memory_space=pltpu.VMEM)] * 2,
        out_specs=(pl.BlockSpec(memory_space=pltpu.VMEM), pl.BlockSpec(memory_space=pltpu.VMEM)),
        scratch_shapes=[pltpu.VMEM((K + R, K), jnp.float32), pltpu.VMEM((NB, NB), jnp.float32),
                        pltpu.VMEM((NB, NB), jnp.float32)],
        compiler_params=pltpu.CompilerParams(vmem_limit_bytes=40 * 2**20),
        name="cholesky_basis",
    )(gram, s)


def project_body(b_ref, wz_ref, m_ref, o_ref, bz, dz, sbuf, rbuf, zsend, zrecv, ysend, yrecv, *, E):
    ch, K = b_ref.shape
    rr, cw = wz_ref.shape
    rows = rr // NY
    e = lax.axis_index("expert")
    f = lax.axis_index("fsdp")
    y = lax.rem(f, NY)
    z = f // NY
    ydev = lambda d: (e, z * NY + lax.rem(y + d + NY, NY))
    zdev = lambda d: (e, lax.rem(z + d + NZ, NZ) * NY + y)
    barrier = pltpu.get_barrier_semaphore()
    partners = [ydev(1), ydev(-1), zdev(1), zdev(-1)]
    for p in partners:
        pl.semaphore_signal(barrier, inc=1, device_id=p, device_id_type=MESH)
    bz[pl.ds(pl.multiple_of(z * ch, 16), ch), :] = b_ref[...]
    pl.semaphore_wait(barrier, len(partners))
    ha = 80
    cs = {}
    def blk(t, r, n):
        return pl.ds(pl.multiple_of(lax.rem(t + NZ, NZ) * ch + r, 16), n)
    def send(dr, s):
        sgn = 1 - 2 * dr
        r, n = (0, ch) if s < 3 else ((0, ha) if dr == 0 else (ha, ch - ha))
        at = bz.at[blk(z - sgn * s, r, n), :]
        c = rc(at, at, zsend.at[dr, s], zrecv.at[dr, s], zdev(sgn))
        c.start()
        cs[dr, s] = c
    send(0, 0); send(1, 0)
    def delta(i, _):
        r = pl.ds(pl.multiple_of(i * 64, 64), 64)
        dz[r, :] = (wz_ref[r, :].astype(jnp.float32) - m_ref[r, :].astype(jnp.float32) * (1.0 / E)).astype(jnp.bfloat16)
        return 0
    lax.fori_loop(0, rr // 64, delta, 0)
    for s in range(1, 4):
        for dr in (0, 1):
            cs[dr, s - 1].wait_recv()
            send(dr, s)
    for dr in (0, 1):
        cs[dr, 3].wait_recv()
    def part(d, r, n):
        yy = lax.rem(y + d + NY, NY)
        return jnp.dot(dz[pl.ds(pl.multiple_of(yy * rows + r, 16), n), :], bz[...], preferred_element_type=jnp.float32)
    h = rows // 2
    ys = {}
    def ysnd(dr, s, r, n):
        c = rc(sbuf.at[dr, s, pl.ds(r, n), :], rbuf.at[dr, s, pl.ds(r, n), :], ysend.at[dr, s], yrecv.at[dr, s],
               ydev(1 - 2 * dr))
        c.start()
        ys[dr, s] = c
    for dr in (0, 1):
        sbuf[dr, 0, h * dr:h * dr + h, :] = part(2, h * dr, h).astype(jnp.bfloat16)
        ysnd(dr, 0, h * dr, h)
    for dr in (0, 1):
        pt = part(1 - 2 * dr, 0, rows)
        a, b = h * dr, h * (1 - dr)
        sbuf[dr, 1, b:b + h, :] = pt[b:b + h].astype(jnp.bfloat16)
        ys[dr, 0].wait_recv()
        sbuf[dr, 1, a:a + h, :] = (pt[a:a + h] + rbuf[dr, 0, a:a + h, :].astype(jnp.float32)).astype(jnp.bfloat16)
        ysnd(dr, 1, 0, rows)
    o_ref[...] = part(0, 0, rows)
    for dr in (0, 1):
        ys[dr, 1].wait_recv()
        o_ref[...] += rbuf[dr, 1].astype(jnp.float32)
    for c in list(cs.values()) + list(ys.values()):
        c.wait_send()

def project_kernel(b, wz, m, E):
    ch, K = b.shape; rr, cw = wz.shape
    rows = rr // NY
    V = pl.BlockSpec(memory_space=pltpu.VMEM)
    DM = pltpu.SemaphoreType.DMA
    return pl.pallas_call(
        functools.partial(project_body, E=E),
        out_shape=jax.ShapeDtypeStruct((rows, K), jnp.float32),
        in_specs=[V, V, V], out_specs=V,
        scratch_shapes=[pltpu.VMEM((ch * NZ, K), jnp.bfloat16), pltpu.VMEM((rr, cw), jnp.bfloat16),
                        pltpu.VMEM((2, 2, rows, K), jnp.bfloat16), pltpu.VMEM((2, 2, rows, K), jnp.bfloat16),
                        DM((2, 4)), DM((2, 4)), DM((2, 2)), DM((2, 2))],
        compiler_params=pltpu.CompilerParams(collective_id=1, has_side_effects=True, vmem_limit_bytes=48 * 2**20),
        name="project_exchange",
    )(b, wz, m)


def on_device(weights, gaussian):
    experts = lax.axis_size("expert")
    d = weights.shape[2]
    own, wz = sketch_kernel(weights[0], gaussian)
    summed = lax.psum(wz, "expert")
    sketch = own - lax.psum(own, "expert") / experts
    gram = lax.psum(jnp.dot(sketch.T, sketch, precision=lax.Precision.HIGHEST), "fsdp")
    orthonormal, basis = chol_basis(gram, sketch, d)
    perm = [(z * NY + y, y * NZ + z) for z in range(NZ) for y in range(NY)]
    placed = lax.ppermute(orthonormal, "fsdp", perm)
    projection = project_kernel(basis, wz, summed, experts)
    return (placed[None], projection[None])


def solution(mesh):
    in_specs = (P("expert", "fsdp", None), P("fsdp", None))
    out_specs = (P("expert", "fsdp", None), P("expert", "fsdp", None))
    return jax.shard_map(
        on_device, mesh=mesh, in_specs=in_specs, out_specs=out_specs, check_vma=False
    )
```

time: 782 us -> 417 us (0.53)
  waiting for transfers between devices: 548 us -> 245 us
  other arithmetic: 157 us -> 1.14 us
  Pallas kernels: 0 us -> 141 us
  matrix products: 34.6 us -> 3 us
  local copies, waits for them, and re-layouts: 18.6 us -> 7.3 us
    reduce_scatter x1 -> x0, waiting for transfers between devices: 236 us -> none  [on_device(): lax.psum_scatter(lax.dot_general(columns, gaussian, (((0,), (0,)), ((), (...]
    another operation x21 -> x0, other arithmetic: 152 us -> none  [the longest x18 101 us: factor_basis(): lower_factor = jnp.linalg.cholesky(gram_matrix)]
    pallas_call x0 -> x3, Pallas kernels: none -> 141 us  [the longest x1 64.7 us: sketch_kernel(): pl.pallas_call(functools.partial(sketch_body, SUBS=subs), out_shape=(jax....]
    all_gather x1 -> x0, waiting for transfers between devices: 84.7 us -> none  [on_device(): lax.all_gather(basis_copy, 'fsdp', axis=0, tiled=True)]
    psum x2 -> x3, waiting for transfers between devices: 227 us -> 244 us  [the longest x1 149 us: on_device(): lax.psum(jnp.dot(sketch.T, sketch, precision=lax.Precision.HIGHEST), 'fsdp')]
    another operation x17 -> x0, matrix products: 16.1 us -> none  [the longest x9 8.69 us: factor_basis(): jax.scipy.linalg.solve_triangular(lower_factor, sketch_part.T, lower=True)]
    dot_general x3 -> x1, matrix products: 18.5 us -> 3 us  [on_device(): jnp.dot(sketch.T, sketch, precision=lax.Precision.HIGHEST)]
    another operation x21 -> x0, local copies, waits for them, and re-layouts: 14 us -> none
  transfers between devices with their start and end apart: 4 -> 4, of which waited for: 4 -> 3; matrix products, arithmetic and copies ran while one was open for 0% -> 0% of each run, Pallas kernels for 0% -> 18%
where the time goes in v1:
time: 417 us
  waiting for transfers between devices  245 us (59%)
  Pallas kernels  141 us (34%)
  between operations  13.8 us (3%)
  local copies, waits for them, and re-layouts  7.3 us (2%)
  starting transfers between devices  4.98 us (1%)
    psum x1, waiting for transfers between devices, on_device(): lax.psum(jnp.dot(sketch.T, sketch, precision=lax.Precision.HIGHEST), 'fsdp')  149 us
    psum x1, waiting for transfers between devices, on_device(): sketch = own - lax.psum(own, 'expert') / experts  64.9 us
    pallas_call x1, Pallas kernels, sketch_kernel(): pl.pallas_call(functools.partial(sketch_body, SUBS=subs), out_shape=(jax....  64.7 us
    pallas_call x1, Pallas kernels, project_kernel(): pl.pallas_call(functools.partial(project_body, E=E), out_shape=jax.ShapeD...  40.8 us
    pallas_call x1, Pallas kernels, chol_basis(): pl.pallas_call(functools.partial(basis_body, K=K, D=D), out_shape=(jax.Sh...  35.8 us
    psum x1, waiting for transfers between devices, on_device(): summed = lax.psum(wz, 'expert')  30.7 us
  transfers between devices with their start and end apart: 4, of which 3 were waited for; matrix products, arithmetic and copies ran while one was open for 0% of the time, Pallas kernels for 18%

profile of v1, /device:TPU:8, one launch (start us, length us, event | category | flops | bytes accessed | tf_op | source)
XLA Modules:
  0.0 416.7 jit_solution(12685218197815629604)
XLA Ops:
  7.2 0.0 all-reduce.4.cloned.1.call-start
  7.2 0.0 copy-start
  7.2 1.7 copy-done
  8.9 0.0 copy-start.3
  8.9 1.0 copy-done.3
  9.8 64.7 %sketch_exchange.1 = (f32[144,640]{1,0:T(8,128)}, bf16[1024,1152]{1,0:T(8,128)(2,1)}) custom-call(bf16[256,4608]{1,0:T(8,128)(2,1)S(1)} %bitcast.6, bf16[256,640]{1,0:T(8,128)(2,1)S(1)} %copy-done.3), custom_call_target="tpu_custom_call" | custom-call | tf_op jit(solution)/shard_map/sketch_exchange/pallas_call | solution.py:122
  74.5 0.0 all-reduce.4.cloned.1.call-update
  74.6 0.0 all-reduce.6.cloned.1.call-start
  74.6 64.9 %all-reduce.4.cloned.1.call-done = f32[144,640]{1,0:T(8,128)} async-done(((f32[144,640]{1,0:T(8,128)}), f32[144,640]{1,0:T(8,128)}) %all-reduce.4.cloned.1.call-update) | async-done | bytes 368656 | tf_op jit(solution)/shard_map/psum | solution.py:306
  139.5 1.1 multiply_subtract_fusion.s_ref
  140.6 3.0 fusion
  143.6 0.0 all-reduce.6.cloned.1.call-update
  143.6 0.0 all-reduce.8.cloned.1.call-start
  143.7 0.7 all-reduce.8.cloned.1.call-update
  144.4 148.9 %all-reduce.6.cloned.1.call-done.gram_ref = f32[640,640]{1,0:T(8,128)} async-done(((f32[640,640]{1,0:T(8,128)}), f32[640,640]{1,0:T(8,128)}) %all-reduce.6.cloned.1.call-update) | async-done | bytes 1638416 | tf_op jit(solution)/shard_map/psum | solution.py:307
  293.3 0.0 copy-start.2
  293.3 1.4 copy-done.2
  294.7 35.8 %cholesky_basis.1 = (f32[144,640]{1,0:T(8,128)S(1)}, bf16[144,640]{1,0:T(8,128)(2,1)S(1)}) custom-call(f32[640,640]{1,0:T(8,128)S(1)} %copy-done.2, f32[144,640]{1,0:T(8,128)S(1)} %multiply_subtract_fusion.s_ref), custom_call_target="tpu_custom_call" | custom-call | tf_op jit(solution)/shard_map/cholesky_basis/pallas_call | solution.py:206
  330.5 4.9 %collective-permute-start = (f32[144,640]{1,0:T(8,128)S(1)}, f32[144,640]{1,0:T(8,128)S(1)}, u32[]{:S(2)}, u32[]{:S(2)}) collective-permute-start(f32[144,640]{1,0:T(8,128)S(1)} %get-tuple-element.7), channel_id=1, source_target_pairs={{0,0},{1,8},{2,16},{3,24},{4,1},{5,9},{6,17},{7,25},{8,2},{9,10},{... | collective-permute-start | bytes 1105928 | tf_op jit(solution)/shard_map/ppermute | solution.py:310
  335.4 30.7 %all-reduce.8.cloned.1.call-done.m_ref = bf16[1024,1152]{1,0:T(8,128)(2,1)} async-done(((bf16[1024,1152]{1,0:T(8,128)(2,1)}), bf16[1024,1152]{1,0:T(8,128)(2,1)}) %all-reduce.8.cloned.1.call-update) | async-done | bytes 2359312 | tf_op jit(solution)/shard_map/psum | solution.py:305
  366.1 0.0 copy-start.1
  366.1 1.7 copy-done.1
  367.7 40.8 %project_exchange.1 = f32[256,640]{1,0:T(8,128)S(1)} custom-call(bf16[144,640]{1,0:T(8,128)(2,1)S(1)} %get-tuple-element.8.b_ref, bf16[1024,1152]{1,0:T(8,128)(2,1)} %get-tuple-element.9.wz_ref, bf16[1024,1152]{1,0:T(8,128)(2,1)S(1)} %copy-done.1), custom_call_target="tpu_custom_call" | custom-call | tf_op jit(solution)/shard_map/project_exchange/pallas_call | solution.py:289
  408.5 0.0 collective-permute-done
  408.6 0.7 copy.9
  409.3 0.8 copy.10
Async XLA Ops:
  7.2 132.3 %all-reduce.4.cloned.1.call-start = ((), (), s32[]{:S(2)}) async-start(), calls=%async_computation | async-start | bytes 737280 | tf_op jit(solution)/shard_map/psum | solution.py:306
  7.2 1.7 copy-start
  8.9 1.0 copy-start.3
  74.6 218.7 %all-reduce.6.cloned.1.call-start = ((), (), s32[]{:S(2)}) async-start(), calls=%async_computation.1 | async-start | bytes 3276800 | tf_op jit(solution)/shard_map/psum | solution.py:307
  143.6 222.4 %all-reduce.8.cloned.1.call-start = ((), (), s32[]{:S(2)}) async-start(), calls=%async_computation.2 | async-start | bytes 4718592 | tf_op jit(solution)/shard_map/psum | solution.py:305
  293.3 1.4 copy-start.2
  330.5 78.0 %collective-permute-start = (f32[144,640]{1,0:T(8,128)S(1)}, f32[144,640]{1,0:T(8,128)S(1)}, u32[]{:S(2)}, u32[]{:S(2)}) collective-permute-start(f32[144,640]{1,0:T(8,128)S(1)} %get-tuple-element.7), channel_id=1, source_target_pairs={{0,0},{1,8},{2,16},{3,24},{4,1},{5,9},{6,17},{7,25},{8,2},{9,10},{... | collective-permute-start | bytes 1105928 | tf_op jit(solution)/shard_map/ppermute | solution.py:310
  366.1 1.7 copy-start.1
Sparse Core Ops, SparseCore 0:
  74.7 64.7 all-reduce.3
  143.8 149.4 all-reduce.5
  295.7 70.3 all-reduce.7

commit v2 on v0

v2 whole, which is shorter than its diff:
```python
import functools
import jax
import jax.numpy as jnp
from jax import lax
from jax.sharding import PartitionSpec as P
from jax.experimental import pallas as pl
from jax.experimental.pallas import tpu as pltpu

MESH = pl.DeviceIdType.MESH
NX, NY, NZ = 4, 4, 8
NB = 128
F32, BF16 = jnp.float32, jnp.bfloat16


def rc(src, dst, ss, rs, dev):
    return pltpu.make_async_remote_copy(src_ref=src, dst_ref=dst, send_sem=ss, recv_sem=rs, device_id=dev,
                                        device_id_type=MESH)


def place():
    e = lax.axis_index("expert")
    f = lax.axis_index("fsdp")
    x, core, y, z = e // 2, lax.rem(e, 2), lax.rem(f, NY), f // NY
    xdev = lambda d: (lax.rem(x + d + NX, NX) * 2 + core, f)
    ydev = lambda d: (e, z * NY + lax.rem(y + d + NY, NY))
    zdev = lambda d: (e, lax.rem(z + d + NZ, NZ) * NY + y)
    return x, core, y, z, xdev, ydev, zdev, (e + 1 - 2 * core, f)


def greet(partners):
    barrier = pltpu.get_barrier_semaphore()
    for p in partners:
        pl.semaphore_signal(barrier, inc=1, device_id=p, device_id_type=MESH)
    pl.semaphore_wait(barrier, len(partners))


def at(start, size, unit):
    return pl.ds(pl.multiple_of(start, unit), size)


def sketch_body(w_ref, g_ref, s_ref, wz_ref, wv, gv, p_ref, sbuf, rbuf, sp, sx, tb, tr, mo, mr,
           wsend, wrecv, gsend, grecv, fsend, frecv, zsend, zrecv, csend, crecv, xsend, xrecv, hsend, hrecv, loc, *, SUBS):
    rows, D = w_ref.shape
    K = g_ref.shape[1]
    cw = D // NY
    ch = cw // NZ
    ex = ch - NB
    x, core, y, z, xdev, ydev, zdev, sib = place()
    greet([ydev(1), ydev(2), ydev(3), sib, zdev(1), zdev(-1), xdev(1), xdev(2), xdev(3)])

    hr = rows // 2
    mine = at(y * rows, rows, rows)
    gcs = []
    for d in (1, 3, 2):
        c = rc(g_ref.at[at(core * hr, hr, hr), :], gv.at[at(y * rows + core * hr, hr, hr), :],
               gsend.at[d], grecv.at[d], ydev(d))
        c.start()
        gcs.append((d, c))
    lg = pltpu.make_async_copy(g_ref, gv.at[mine, :], loc.at[0])
    lg.start()
    seq = [NZ] + [lax.rem(z + k + 2 * NZ, NZ) for k in (4, 3, 5, 2, 6, 1, 7, 0)]
    wcs = []
    lws = []
    for k, b in enumerate(seq):
        lw = pltpu.make_async_copy(w_ref.at[:, at(y * cw + b * NB, NB, NB)], wv.at[mine, at(b * NB, NB, NB)], loc.at[2 + k])
        lw.start()
        lws.append(lw)
        now = []
        for d in (1, 3, 2):
            yy = lax.rem(y + d, NY)
            c = rc(w_ref.at[:, at(yy * cw + b * NB, NB, NB)], wv.at[mine, at(b * NB, NB, NB)],
                   wsend.at[k, d], wrecv.at[k, d], ydev(d))
            c.start()
            now.append(c)
        wcs.append(now)
    fcs = []
    for d, c in gcs:
        c.wait_recv()
        piece = at(lax.rem(y - d + NY, NY) * rows + core * hr, hr, hr)
        h = rc(gv.at[piece, :], gv.at[piece, :], fsend.at[d], frecv.at[d], sib)
        h.start()
        fcs.append(h)
    lg.wait()
    for h in fcs:
        h.wait_recv()

    def product(k):
        lws[k].wait()
        for c in wcs[k]:
            c.wait_recv()
        o = at(seq[k] * NB, NB, NB)
        p_ref[o, :] = lax.dot_general(wv[:, o], gv[...], (((0,), (0,)), ((), ())), preferred_element_type=F32)

    ha = 64
    prev = {}

    def own(t, r, n, c0, c1):
        if r < NB:
            head = p_ref[at(t * NB + r, min(n, NB - r), 16), c0:c1]
            if r + n <= NB:
                return head
            return jnp.concatenate([head, p_ref[at(NZ * NB + t * ex, ex, 16), c0:c1]], axis=0)

    product(0)
    for s in range(4):
        for k in ((1,), (2, 3), (4, 5), (6, 7))[s]:
            product(k)
        for u, (c0, c1) in enumerate(SUBS):
            for dr, sgn in ((0, 1), (1, -1)):
                t = lax.rem(z + sgn * (4 - s) + NZ, NZ)
                a, m = (0, ha) if dr == 0 else (ha, ch - ha)
                q, l = (ha, ch - ha) if dr == 0 else (0, ha)
                if s:
                    prev[dr, u].wait_recv()
                if s == 0:
                    sbuf[dr, s, a:a + m, c0:c1] = own(t, a, m, c0, c1).astype(BF16)
                    r, n = a, m
                elif s == 1:
                    sbuf[dr, s, a:a + m, c0:c1] = (own(t, a, m, c0, c1) + rbuf[dr, 0, a:a + m, c0:c1].astype(F32)).astype(BF16)
                    sbuf[dr, s, q:q + l, c0:c1] = own(t, q, l, c0, c1).astype(BF16)
                    r, n = 0, ch
                else:
                    sbuf[dr, s, :, c0:c1] = (own(t, 0, ch, c0, c1) + rbuf[dr, s - 1, :, c0:c1].astype(F32)).astype(BF16)
                    r, n = 0, ch
                if s:
                    prev[dr, u].wait_send()
                c = rc(sbuf.at[dr, s, pl.ds(r, n), pl.ds(c0, c1 - c0)], rbuf.at[dr, s, pl.ds(r, n), pl.ds(c0, c1 - c0)],
                       zsend.at[dr, s, u], zrecv.at[dr, s, u], zdev(sgn))
                c.start()
                prev[dr, u] = c
    product(8)
    out = pltpu.make_async_copy(wv, wz_ref, loc.at[1])
    out.start()
    hm = 80
    half = at((ch - hm) * core, hm, 16)
    pairs = []
    for u, (c0, c1) in enumerate(SUBS):
        prev[0, u].wait()
        prev[1, u].wait()
        sp[:, c0:c1] = (own(z, 0, ch, c0, c1) + rbuf[0, 3, :, c0:c1].astype(F32) + rbuf[1, 3, :, c0:c1].astype(F32))
        c = rc(sp.at[:, pl.ds(c0, c1 - c0)], sx.at[:, pl.ds(c0, c1 - c0)], csend.at[u], crecv.at[u], sib)
        c.start()
        pairs.append(c)
    xs = []
    for u, (c0, c1) in enumerate(SUBS):
        pairs[u].wait_recv()
        mo[:, c0:c1] = sp[half, c0:c1] + sx[half, c0:c1]
        tb[:, c0:c1] = mo[:, c0:c1].astype(BF16)
        now = []
        for d in (1, 3, 2):
            c = rc(tb.at[:, pl.ds(c0, c1 - c0)], tr.at[d, :, pl.ds(c0, c1 - c0)], xsend.at[u, d], xrecv.at[u, d], xdev(d))
            c.start()
            now.append(c)
        xs.append(now)
    hs = []
    for u, (c0, c1) in enumerate(SUBS):
        for c in xs[u]:
            c.wait_recv()
        mo[:, c0:c1] = (mo[:, c0:c1] + tr[1, :, c0:c1].astype(F32) + tr[2, :, c0:c1].astype(F32)
                        + tr[3, :, c0:c1].astype(F32)) * (1.0 / (2 * NX))
        h = rc(mo.at[:, pl.ds(c0, c1 - c0)], mr.at[:, pl.ds(c0, c1 - c0)], hsend.at[u], hrecv.at[u], sib)
        h.start()
        hs.append(h)
        s_ref[half, c0:c1] = sp[half, c0:c1] - mo[:, c0:c1]
    rest = at(hm * (1 - core), ch - hm, 16)
    for u, (c0, c1) in enumerate(SUBS):
        hs[u].wait_recv()
        s_ref[rest, c0:c1] = sp[rest, c0:c1] - mr[at((2 * hm - ch) * (1 - core), ch - hm, 16), c0:c1]
    for c in [c for _, c in gcs] + fcs + [c for now in wcs + xs for c in now] + pairs + hs:
        c.wait_send()
    out.wait()


def sketch_kernel(w, g, subs=((0, 384), (384, 640))):
    rows, D = w.shape
    K = g.shape[1]
    cw = D // NY
    ch = cw // NZ
    nu = len(subs)
    V = pl.BlockSpec(memory_space=pltpu.VMEM)
    A = pl.BlockSpec(memory_space=pl.ANY)
    DM = pltpu.SemaphoreType.DMA
    M = pltpu.VMEM
    return pl.pallas_call(
        functools.partial(sketch_body, SUBS=subs),
        out_shape=(jax.ShapeDtypeStruct((ch, K), F32), jax.ShapeDtypeStruct((rows * NY, cw), BF16)),
        in_specs=[A, A], out_specs=(V, A),
        scratch_shapes=[M((rows * NY, cw), BF16), M((rows * NY, K), BF16), M((cw, K), F32),
                        M((2, 4, ch, K), BF16), M((2, 4, ch, K), BF16),
                        M((ch, K), F32), M((ch, K), F32), M((80, K), BF16), M((4, 80, K), BF16), M((80, K), F32), M((80, K), F32),
                        DM((9, 4)), DM((9, 4)), DM((4,)), DM((4,)), DM((4,)), DM((4,)),
                        DM((2, 4, nu)), DM((2, 4, nu)), DM((nu,)), DM((nu,)), DM((nu, 4)), DM((nu, 4)), DM((nu,)), DM((nu,)),
                        DM((11,))],
        compiler_params=pltpu.CompilerParams(collective_id=0, has_side_effects=True, vmem_limit_bytes=48 * 2**20),
        name="sketch_exchange",
    )(w, g)


HI = lax.Precision.HIGHEST
GROUPS = ((0, 768), (768, 1280))
STACK = 2048


def base_inverse(t_ref, n_ref):
    sub = lax.broadcasted_iota(jnp.int32, (8, NB), 0)
    row = lax.broadcasted_iota(jnp.int32, (NB, NB), 0)
    col = lax.broadcasted_iota(jnp.int32, (NB, NB), 1)
    n_ref[...] = jnp.where(row == col, 1.0, 0.0).astype(F32)
    nsub = NB // 8
    wide = lambda v: jnp.broadcast_to(v, (8, NB))
    cur_t, cur_n = t_ref[0:8, :], n_ref[0:8, :]
    for b in range(nsub):
        r0 = 8 * b
        last = b == nsub - 1
        c = [wide(cur_t[:, r0 + i:r0 + i + 1]) for i in range(8)]
        if not last:
            nt, nn = t_ref[r0 + 8:r0 + 16, :], n_ref[r0 + 8:r0 + 16, :]
            d = [wide(nt[:, r0 + i:r0 + i + 1]) for i in range(8)]
        for i in range(8):
            rs = lax.rsqrt(wide(c[i][i:i + 1, :]))
            m = c[i] * rs
            mk = {}
            for k in range(i + 1, 8):
                mk[k] = wide(m[k:k + 1, :])
                c[k] = c[k] - m * mk[k]
            mm = jnp.where(sub > i, m, 0.0)
            ft = wide(cur_t[i:i + 1, :]) * rs
            fn = wide(cur_n[i:i + 1, :]) * rs
            cur_t = jnp.where(sub == i, ft, cur_t - mm * ft)
            cur_n = jnp.where(sub == i, fn, cur_n - mm * fn)
            if not last:
                md = d[i] * rs
                for k in range(i + 1, 8):
                    d[k] = d[k] - md * mk[k]
                nt = nt - md * ft
                nn = nn - md * fn
        n_ref[r0:r0 + 8, :] = cur_n
        if not last:
            if b < nsub - 2:
                both = jnp.concatenate([cur_t, cur_n], axis=1)
                upd = lax.dot_general(cur_t, both, (((0,), (0,)), ((), ())), precision=HI, preferred_element_type=F32)
                t_ref[r0 + 16:, :] = t_ref[r0 + 16:, :] - upd[r0 + 16:, :NB]
                n_ref[r0 + 16:, :] = n_ref[r0 + 16:, :] - upd[r0 + 16:, NB:]
            cur_t, cur_n = nt, nn


def basis_body(s_ref, wz_ref, orth_ref, proj_ref, gp, gr, yr0, yr1, yb0, yb1, zr0, zr1, qf0, qf1,
           fw, fb, fr, mw, dz, x_ref, t_ref, n_ref, bc, bn, ysb, yrb, ob,
           f1s, f1r, f2s, f2r, f3s, f3r, f4s, f4r, ys1, yr1s, zs1, zr1s, zs2, zr2s, ys2, yr2s,
           bs, br, ps, pr, os_, or_):
    ch, K = s_ref.shape
    rr, cw = wz_ref.shape
    rows = rr // NY
    D = cw * NY
    nb = K // NB
    ex = ch - NB
    x, core, y, z, xdev, ydev, zdev, sib = place()
    zd = (1, 7, 2, 6, 3, 5, 4)
    yd = (1, 3, 2)
    greet([ydev(d) for d in yd] + [zdev(d) for d in zd] + [xdev(d) for d in yd] + [sib])

    hf = rr // 2
    f1 = rc(wz_ref.at[at(hf * (1 - core), hf, hf), :], fw, f1s.at[0], f1r.at[0], sib)
    f1.start()
    r0 = 0
    starts = []
    for j in range(nb):
        n = K - j * NB
        gp[r0:r0 + n, :] = lax.dot_general(s_ref[:, j * NB:], s_ref[:, j * NB:(j + 1) * NB], (((0,), (0,)), ((), ())),
                                           precision=HI, preferred_element_type=F32)
        starts.append(r0)
        r0 += n
    gp[r0:, :] = jnp.zeros((STACK - r0, NB), F32)
    done = [f1]
    yrg, ybg, zrg, qfg = (yr0, yr1), (yb0, yb1), (zr0, zr1), (qf0, qf1)
    p1 = []
    for g, (a, n) in enumerate(GROUPS):
        q = n // NY
        now = []
        for d in yd:
            yy = lax.rem(y + d, NY)
            c = rc(gp.at[at(a + q * yy, q, 8), :], yrg[g].at[d], ys1.at[g, d], yr1s.at[g, d], ydev(d))
            c.start()
            now.append(c)
        p1.append(now)
    f1.wait_recv()
    step = 64

    def pair(i, _):
        o = at(i * step, step, step)
        fb[o, :] = (wz_ref[at(hf * core + i * step, step, step), :].astype(F32) + fw[o, :].astype(F32)).astype(BF16)
        return 0
    lax.fori_loop(0, hf // step, pair, 0)
    qx = hf // NX
    f2 = []
    for d in yd:
        xx = lax.rem(x + d, NX)
        c = rc(fb.at[at(qx * xx, qx, qx), :], fr.at[d], f2s.at[d], f2r.at[d], xdev(d))
        c.start()
        f2.append(c)
    p2 = []
    for g, (a, n) in enumerate(GROUPS):
        q = n // NY
        m = q // NZ
        for c in p1[g]:
            c.wait_recv()
        ybg[g][...] = gp[at(a + q * y, q, 8), :] + yrg[g][1] + yrg[g][2] + yrg[g][3]
        now = []
        for d in zd:
            zz = lax.rem(z + d, NZ)
            c = rc(ybg[g].at[at(m * zz, m, 8), :], zrg[g].at[d], zs1.at[g, d], zr1s.at[g, d], zdev(d))
            c.start()
            now.append(c)
        p2.append(now)
    p3 = []
    for g, (a, n) in enumerate(GROUPS):
        m = n // NY // NZ
        for c in p2[g]:
            c.wait_recv()
        here = at(m * z, m, 8)
        tot = ybg[g][here, :]
        for d in range(1, NZ):
            tot = tot + zrg[g][d]
        qfg[g][here, :] = tot * (1.0 / D)
        now = []
        for d in zd:
            c = rc(qfg[g].at[here, :], qfg[g].at[here, :], zs2.at[g, d], zr2s.at[g, d], zdev(d))
            c.start()
            now.append(c)
        p3.append(now)
    for c in f2:
        c.wait_recv()
    mine = at(hf * core + qx * x, qx, qx)

    def four(i, _):
        o = at(i * 32, 32, 32)
        mw[at(hf * core + qx * x + i * 32, 32, 32), :] = (
            fb[at(qx * x + i * 32, 32, 32), :].astype(F32) + fr[1, o, :].astype(F32) + fr[2, o, :].astype(F32)
            + fr[3, o, :].astype(F32)).astype(BF16)
        return 0
    lax.fori_loop(0, qx // 32, four, 0)
    f3 = []
    for d in yd:
        c = rc(mw.at[mine, :], mw.at[mine, :], f3s.at[d], f3r.at[d], xdev(d))
        c.start()
        f3.append(c)
    p4 = []
    for g, (a, n) in enumerate(GROUPS):
        q = n // NY
        for c in p3[g]:
            c.wait_recv()
        here = at(a + q * y, q, 8)
        now = []
        for d in yd:
            c = rc(qfg[g], gr.at[here, :], ys2.at[g, d], yr2s.at[g, d], ydev(d))
            c.start()
            now.append(c)
        gr[here, :] = qfg[g][...]
        p4.append(now)
    for c in f3:
        c.wait_recv()
    f4 = rc(mw.at[at(hf * core, hf, hf), :], mw.at[at(hf * core, hf, hf), :], f4s.at[0], f4r.at[0], sib)
    f4.start()
    f4.wait_recv()

    def delta(i, _):
        o = at(i * step, step, step)
        dz[o, :] = (wz_ref[o, :].astype(F32) - mw[o, :].astype(F32) * (1.0 / (2 * NX))).astype(BF16)
        return 0
    lax.fori_loop(0, rr // step, delta, 0)
    done += f2 + f3 + [f4] + [c for ph in (p1, p2, p3, p4) for now in ph for c in now]

    x_ref[0:K, :] = jnp.zeros((K, K), F32)
    x_ref[K:K + ch, :] = s_ref[...]
    for c in p4[0]:
        c.wait_recv()
    x_ref[0:K, 0:NB] = gr[0:K, :]

    def basis_copy(j, d):
        cols = at(j * NB, NB, NB)
        return rc(bc.at[z, :, cols], bc.at[z, :, cols], bs.at[j, d], br.at[j, d], zdev(d))

    def part_copy(j, d):
        cols = at(j * NB, NB, NB)
        return rc(ysb.at[d, :, cols], yrb.at[d, :, cols], ps.at[j, d], pr.at[j, d], ydev(d))

    ysrc = z // 2

    def orth_copy(j, d):
        cols = at(j * NB, NB, NB)
        t = 4 * lax.rem(z, 2) + lax.rem(y + d, NY)
        return rc(bn.at[at(t * ch, ch, 16), cols], ob.at[:, cols], os_.at[j, d], or_.at[j], ydev(d))

    def factor(j):
        cols = at(j * NB, NB, NB)
        t_ref[...] = x_ref[cols, cols]
        base_inverse(t_ref, n_ref)
        p = lax.dot_general(x_ref[:, cols], n_ref[...], (((1,), (1,)), ((), ())), precision=HI,
                            preferred_element_type=F32)
        bc[z, :, cols] = p[K:K + ch].astype(BF16)
        for d in zd:
            basis_copy(j, d).start()
        r = lax.broadcasted_iota(jnp.int32, (K, NB), 0)
        lk = jnp.where(r >= (j + 1) * NB, p[0:K], 0.0)

        @pl.when(j < nb - 1)
        def _():
            x_ref[...] = x_ref[...] - lax.dot_general(p, lk, (((1,), (1,)), ((), ())), precision=HI,
                                                      preferred_element_type=F32)

    def project(j):
        cols = at(j * NB, NB, NB)
        for d in zd:
            basis_copy(j, d).wait_recv()
        for t in range(NZ):
            bn[t * NB:(t + 1) * NB, cols] = bc[t, 0:NB, cols]
            bn[NZ * NB + t * ex:NZ * NB + (t + 1) * ex, cols] = bc[t, NB:ch, cols]
        for d in (2, 1, 3):
            yy = lax.rem(y + d, NY)
            ysb[d, :, cols] = jnp.dot(dz[at(yy * rows, rows, rows), :], bn[:, cols],
                                      preferred_element_type=F32).astype(BF16)
            part_copy(j, d).start()

        @pl.when(y == ysrc)
        def _():
            for d in yd:
                orth_copy(j, d).start()
            t = 4 * lax.rem(z, 2) + y
            ob[:, cols] = bn[at(t * ch, ch, 16), cols]
        proj_ref[:, cols] = jnp.dot(dz[at(y * rows, rows, rows), :], bn[:, cols], preferred_element_type=F32)

    def finish(j):
        cols = at(j * NB, NB, NB)
        for d in yd:
            part_copy(j, d).wait_recv()
        proj_ref[:, cols] += (yrb[1, :, cols].astype(F32) + yrb[2, :, cols].astype(F32) + yrb[3, :, cols].astype(F32))

        @pl.when(y != ysrc)
        def _():
            orth_copy(j, 1).wait_recv()
        orth_ref[:, cols] = ob[:, cols].astype(F32)

    def column(j, _):
        @pl.when(j == 1)
        def _():
            for c in p4[1]:
                c.wait_recv()
            for k in range(1, nb):
                n = K - k * NB
                x_ref[k * NB:K, k * NB:(k + 1) * NB] += gr[starts[k]:starts[k] + n, :]

        @pl.when(j < nb)
        def _():
            factor(j)

        @pl.when(j >= 1)
        def _():
            project(j - 1)

        @pl.when(j >= 2)
        def _():
            finish(j - 2)
        return 0
    lax.fori_loop(0, nb + 1, column, 0)
    finish(nb - 1)

    for c in done:
        c.wait_send()

    def drain(j, _):
        for d in zd:
            basis_copy(j, d).wait_send()
        for d in yd:
            part_copy(j, d).wait_send()

        @pl.when(y == ysrc)
        def _():
            for d in yd:
                orth_copy(j, d).wait_send()
        return 0
    lax.fori_loop(0, nb, drain, 0)


def basis_project_kernel(s, wz):
    ch, K = s.shape
    rr, cw = wz.shape
    rows = rr // NY
    V = pl.BlockSpec(memory_space=pltpu.VMEM)
    DM = pltpu.SemaphoreType.DMA
    M = pltpu.VMEM
    (_, n0), (_, n1) = GROUPS
    q0, q1 = n0 // NY, n1 // NY
    nb = K // NB
    return pl.pallas_call(
        basis_body,
        out_shape=(jax.ShapeDtypeStruct((ch, K), F32), jax.ShapeDtypeStruct((rows, K), F32)),
        in_specs=[V, V], out_specs=(V, V),
        scratch_shapes=[M((STACK, NB), F32), M((STACK, NB), F32), M((NY, q0, NB), F32), M((NY, q1, NB), F32),
                        M((q0, NB), F32), M((q1, NB), F32), M((NZ, q0 // NZ, NB), F32), M((NZ, q1 // NZ, NB), F32),
                        M((q0, NB), F32), M((q1, NB), F32),
                        M((rr // 2, cw), BF16), M((rr // 2, cw), BF16), M((NX, rr // 2 // NX, cw), BF16),
                        M((rr, cw), BF16), M((rr, cw), BF16), M((K + ch, K), F32), M((NB, NB), F32), M((NB, NB), F32),
                        M((NZ, ch, K), BF16), M((cw, K), BF16), M((NY, rows, K), BF16), M((NY, rows, K), BF16), M((ch, K), BF16),
                        DM((1,)), DM((1,)), DM((4,)), DM((4,)), DM((4,)), DM((4,)), DM((1,)), DM((1,)),
                        DM((2, 4)), DM((2, 4)), DM((2, 8)), DM((2, 8)), DM((2, 8)), DM((2, 8)), DM((2, 4)), DM((2, 4)),
                        DM((nb, 8)), DM((nb, 8)), DM((nb, 4)), DM((nb, 4)), DM((nb, 4)), DM((nb,))],
        compiler_params=pltpu.CompilerParams(collective_id=1, has_side_effects=True, vmem_limit_bytes=56 * 2**20),
        name="basis_project",
    )(s, wz)


def on_device(weights, gaussian):
    sketch, exchanged = sketch_kernel(weights[0], gaussian)
    orthonormal, projection = basis_project_kernel(sketch, exchanged)
    return (orthonormal[None], projection[None])


def solution(mesh):
    in_specs = (P("expert", "fsdp", None), P("fsdp", None))
    out_specs = (P("expert", "fsdp", None), P("expert", "fsdp", None))
    return jax.shard_map(
        on_device, mesh=mesh, in_specs=in_specs, out_specs=out_specs, check_vma=False
    )
```

time: 782 us -> 166 us (0.21)
  the two profiles are of different devices: /device:TPU:8 before, /device:TPU:1 now
where the time goes in v2:
time: 166 us
  Pallas kernels  157 us (95%)
  local copies, waits for them, and re-layouts  8.49 us (5%)
    pallas_call x1, Pallas kernels, basis_project_kernel(): pl.pallas_call(basis_body, out_shape=(jax.ShapeDtypeStruct((ch, K), F32),...  98.8 us
    pallas_call x1, Pallas kernels, sketch_kernel(): pl.pallas_call(functools.partial(sketch_body, SUBS=subs), out_shape=(jax....  58.2 us
    unnamed x10, local copies, waits for them, and re-layouts  8.49 us

profile of v2, /device:TPU:1, one launch (start us, length us, event | category | flops | bytes accessed | tf_op | source)
XLA Modules:
  0.0 166.2 jit_solution(13694808597862898862)
XLA Ops:
  0.6 0.0 copy-start
  0.6 1.7 copy-done
  2.3 0.0 copy-start.3
  2.3 1.0 copy-done.3
  3.3 58.2 %sketch_exchange.1 = (f32[144,640]{1,0:T(8,128)S(1)}, bf16[1024,1152]{1,0:T(8,128)(2,1)S(1)}) custom-call(bf16[256,4608]{1,0:T(8,128)(2,1)S(1)} %bitcast.3, bf16[256,640]{1,0:T(8,128)(2,1)S(1)} %copy-done.3), custom_call_target="tpu_custom_call" | custom-call | tf_op jit(solution)/shard_map/sketch_exchange/pallas_call | solution.py:184
  61.5 0.0 copy-start.1
  61.5 1.4 copy-done.1
  62.9 0.0 copy-start.2
  62.9 0.7 copy-done.2
  63.6 98.8 %basis_project.1 = (f32[144,640]{1,0:T(8,128)}, f32[256,640]{1,0:T(8,128)}) custom-call(f32[144,640]{1,0:T(8,128)} %copy-done.2, bf16[1024,1152]{1,0:T(8,128)(2,1)} %copy-done.1), custom_call_target="tpu_custom_call" | custom-call | tf_op jit(solution)/shard_map/basis_project/pallas_call | solution.py:494
  162.5 1.7 %copy.6 = f32[1,144,640]{2,1,0:T(8,128)} copy(f32[1,144,640]{2,1,0:T(8,128)} %bitcast.5) | data formatting | bytes 737280
  164.2 2.0 %copy.7 = f32[1,256,640]{2,1,0:T(8,128)} copy(f32[1,256,640]{2,1,0:T(8,128)} %bitcast.4) | data formatting | bytes 1310720
Async XLA Ops:
  0.6 1.7 %copy-start = (bf16[1,256,4608]{2,1,0:T(8,128)(2,1)S(1)}, bf16[1,256,4608]{2,1,0:T(8,128)(2,1)}, u32[]{:S(2)}) copy-start(bf16[1,256,4608]{2,1,0:T(8,128)(2,1)} %param.2) | copy-start | bytes 7077892
  2.3 1.0 copy-start.3
  61.5 1.4 copy-start.1
  62.9 0.7 copy-start.2

commit v3 on v0

v3 whole, which is shorter than its diff:
```python
import jax
import jax.numpy as jnp
from jax import lax
from jax.sharding import PartitionSpec as P
from jax.experimental import pallas as pl
from jax.experimental.pallas import tpu as pltpu

MESH = pl.DeviceIdType.MESH
NX, NY, NZ = 4, 4, 8
NB = 128
F32, BF16 = jnp.float32, jnp.bfloat16
HI = lax.Precision.HIGHEST
SUBS = ((0, 256), (256, 640))
GROUPS = ((0, 256), (256, 512), (768, 512), (1280, 768))
STACK = 2048
AHEAD = 3
YD = (1, 3, 2)
ZD = (1, 7, 2, 6, 3, 5, 4)


def rc(src, dst, ss, rs, dev):
    return pltpu.make_async_remote_copy(src_ref=src, dst_ref=dst, send_sem=ss, recv_sem=rs, device_id=dev,
                                        device_id_type=MESH)


def at(start, size, unit):
    return pl.ds(pl.multiple_of(start, unit), size)


def base_inverse(t_ref, n_ref):
    sub = lax.broadcasted_iota(jnp.int32, (8, NB), 0)
    row = lax.broadcasted_iota(jnp.int32, (NB, NB), 0)
    col = lax.broadcasted_iota(jnp.int32, (NB, NB), 1)
    n_ref[...] = jnp.where(row == col, 1.0, 0.0).astype(F32)
    nsub = NB // 8
    wide = lambda v: jnp.broadcast_to(v, (8, NB))
    cur_t, cur_n = t_ref[0:8, :], n_ref[0:8, :]
    for b in range(nsub):
        r0 = 8 * b
        last = b == nsub - 1
        c = [wide(cur_t[:, r0 + i:r0 + i + 1]) for i in range(8)]
        if not last:
            nt, nn = t_ref[r0 + 8:r0 + 16, :], n_ref[r0 + 8:r0 + 16, :]
            d = [wide(nt[:, r0 + i:r0 + i + 1]) for i in range(8)]
        for i in range(8):
            rs = lax.rsqrt(wide(c[i][i:i + 1, :]))
            m = c[i] * rs
            mk = {}
            for k in range(i + 1, 8):
                mk[k] = wide(m[k:k + 1, :])
                c[k] = c[k] - m * mk[k]
            mm = jnp.where(sub > i, m, 0.0)
            ft = wide(cur_t[i:i + 1, :]) * rs
            fn = wide(cur_n[i:i + 1, :]) * rs
            cur_t = jnp.where(sub == i, ft, cur_t - mm * ft)
            cur_n = jnp.where(sub == i, fn, cur_n - mm * fn)
            if not last:
                md = d[i] * rs
                for k in range(i + 1, 8):
                    d[k] = d[k] - md * mk[k]
                nt = nt - md * ft
                nn = nn - md * fn
        n_ref[r0:r0 + 8, :] = cur_n
        if not last:
            if b < nsub - 2:
                both = jnp.concatenate([cur_t, cur_n], axis=1)
                upd = lax.dot_general(cur_t, both, (((0,), (0,)), ((), ())), precision=HI, preferred_element_type=F32)
                t_ref[r0 + 16:, :] = t_ref[r0 + 16:, :] - upd[r0 + 16:, :NB]
                n_ref[r0 + 16:, :] = n_ref[r0 + 16:, :] - upd[r0 + 16:, NB:]
            cur_t, cur_n = nt, nn


def body(w_ref, g_ref, out_ref,
         wv, gv, p_ref, sbuf, rbuf, sp, sx, tb, tr, mo, mr, s_ref,
         gp, gr, yrv, ybv, zrv, qfv,
         fw, fb, fr, mw, dz, x_ref, l_ref, ln_ref, t_ref, bc, bn, ysb, yrb, ob,
         wsend, wrecv, gsend, grecv, gxsend, gxrecv, fsend, frecv, zsend, zrecv, csend, crecv, xsend, xrecv, hsend, hrecv,
         loc, f1s, f1r, f2s, f2r, f3s, f3r, f4s, f4r, ys1, yr1, zs1, zr1, zs2, zr2, ys2, yr2, bs, br, ps, pr, os_, or_):
    rows, D = w_ref.shape
    K = g_ref.shape[1]
    cw = D // NY
    ch = cw // NZ
    ex = ch - NB
    rr = rows * NY
    nb = K // NB
    e = lax.axis_index("expert")
    f = lax.axis_index("fsdp")
    x, core, y, z = e // 2, lax.rem(e, 2), lax.rem(f, NY), f // NY
    xdev = lambda d: (lax.rem(x + d, NX) * 2 + core, f)
    ydev = lambda d: (e, z * NY + lax.rem(y + d, NY))
    zdev = lambda d: (e, lax.rem(z + d, NZ) * NY + y)
    sib = (e + 1 - 2 * core, f)

    lg = pltpu.make_async_copy(g_ref, gv.at[at(y * rows, rows, rows), :], loc.at[0])
    lg.start()
    barrier = pltpu.get_barrier_semaphore()
    partners = [ydev(d) for d in YD] + [zdev(d) for d in ZD] + [xdev(d) for d in YD] + [sib]
    for p in partners:
        pl.semaphore_signal(barrier, inc=1, device_id=p, device_id_type=MESH)
    pl.semaphore_wait(barrier, len(partners))

    hr, qr = rows // 2, rows // 8
    mine = at(y * rows, rows, rows)
    mypart = core * hr + x * qr
    done = []
    gcs = []
    for d in YD:
        c = rc(g_ref.at[at(mypart, qr, qr), :], gv.at[at(y * rows + mypart, qr, qr), :], gsend.at[d], grecv.at[d], ydev(d))
        c.start()
        gcs.append(c)
    seq = [NZ] + [lax.rem(z + k, NZ) for k in (4, 3, 5, 2, 6, 1, 7, 0)]
    wcs, lws = [], []
    for k, b in enumerate(seq):
        lw = pltpu.make_async_copy(w_ref.at[:, at(y * cw + b * NB, NB, NB)], wv.at[mine, at(b * NB, NB, NB)], loc.at[1 + k])
        lw.start()
        lws.append(lw)
        now = []
        for d in YD:
            yy = lax.rem(y + d, NY)
            c = rc(w_ref.at[:, at(yy * cw + b * NB, NB, NB)], wv.at[mine, at(b * NB, NB, NB)],
                   wsend.at[k, d], wrecv.at[k, d], ydev(d))
            c.start()
            now.append(c)
        wcs.append(now)
    gxs = []
    for i, d in enumerate(YD):
        gcs[i].wait_recv()
        piece = at(lax.rem(y - d + NY, NY) * rows + mypart, qr, qr)
        for dx in YD:
            c = rc(gv.at[piece, :], gv.at[piece, :], gxsend.at[d, dx], gxrecv.at[d, dx], xdev(dx))
            c.start()
            gxs.append(c)
    fcs = []
    for i, d in enumerate(YD):
        for c in gxs[3 * i:3 * i + 3]:
            c.wait_recv()
        piece = at(lax.rem(y - d + NY, NY) * rows + core * hr, hr, hr)
        c = rc(gv.at[piece, :], gv.at[piece, :], fsend.at[d], frecv.at[d], sib)
        c.start()
        fcs.append(c)
    lg.wait()
    for c in fcs:
        c.wait_recv()

    def product(k):
        lws[k].wait()
        for c in wcs[k]:
            c.wait_recv()
        o = at(seq[k] * NB, NB, NB)
        p_ref[o, :] = lax.dot_general(wv[:, o], gv[...], (((0,), (0,)), ((), ())), preferred_element_type=F32)

    ha = 64
    prev = {}

    def own(t, r, n, c0, c1):
        head = p_ref[at(t * NB + r, min(n, NB - r), 16), c0:c1]
        if r + n <= NB:
            return head
        return jnp.concatenate([head, p_ref[at(NZ * NB + t * ex, ex, 16), c0:c1]], axis=0)

    product(0)
    for s in range(4):
        for k in ((1,), (2, 3), (4, 5), (6, 7))[s]:
            product(k)
        for u, (c0, c1) in enumerate(SUBS):
            for dr, d in ((0, 1), (1, NZ - 1)):
                t = lax.rem(z + (4 - s if dr == 0 else NZ - 4 + s), NZ)
                a, m = (0, ha) if dr == 0 else (ha, ch - ha)
                q, l = (ha, ch - ha) if dr == 0 else (0, ha)
                if s:
                    prev[dr, u].wait_recv()
                if s == 0:
                    sbuf[dr, s, a:a + m, c0:c1] = own(t, a, m, c0, c1).astype(BF16)
                    r, n = a, m
                elif s == 1:
                    sbuf[dr, s, a:a + m, c0:c1] = (own(t, a, m, c0, c1) + rbuf[dr, 0, a:a + m, c0:c1].astype(F32)).astype(BF16)
                    sbuf[dr, s, q:q + l, c0:c1] = own(t, q, l, c0, c1).astype(BF16)
                    r, n = 0, ch
                else:
                    sbuf[dr, s, :, c0:c1] = (own(t, 0, ch, c0, c1) + rbuf[dr, s - 1, :, c0:c1].astype(F32)).astype(BF16)
                    r, n = 0, ch
                c = rc(sbuf.at[dr, s, pl.ds(r, n), pl.ds(c0, c1 - c0)], rbuf.at[dr, s, pl.ds(r, n), pl.ds(c0, c1 - c0)],
                       zsend.at[dr, s, u], zrecv.at[dr, s, u], zdev(d))
                c.start()
                done.append(c)
                prev[dr, u] = c
    product(8)
    hm = 80
    half = at((ch - hm) * core, hm, 16)
    rest = at(hm * (1 - core), ch - hm, 16)
    pairs = []
    for u, (c0, c1) in enumerate(SUBS):
        prev[0, u].wait_recv()
        prev[1, u].wait_recv()
        sp[:, c0:c1] = (own(z, 0, ch, c0, c1) + rbuf[0, 3, :, c0:c1].astype(F32) + rbuf[1, 3, :, c0:c1].astype(F32))
        c = rc(sp.at[:, pl.ds(c0, c1 - c0)], sx.at[:, pl.ds(c0, c1 - c0)], csend.at[u], crecv.at[u], sib)
        c.start()
        pairs.append(c)
    hf = rr // 2
    f1 = rc(wv.at[at(hf * (1 - core), hf, hf), :], fw, f1s.at[0], f1r.at[0], sib)
    xs = []
    for u, (c0, c1) in enumerate(SUBS):
        pairs[u].wait_recv()
        mo[:, c0:c1] = sp[half, c0:c1] + sx[half, c0:c1]
        tb[:, c0:c1] = mo[:, c0:c1].astype(BF16)
        now = []
        for d in YD:
            c = rc(tb.at[:, pl.ds(c0, c1 - c0)], tr.at[d, :, pl.ds(c0, c1 - c0)], xsend.at[u, d], xrecv.at[u, d], xdev(d))
            c.start()
            now.append(c)
        xs.append(now)
    f1.start()
    hs = []
    for u, (c0, c1) in enumerate(SUBS):
        for c in xs[u]:
            c.wait_recv()
        mo[:, c0:c1] = (mo[:, c0:c1] + tr[1, :, c0:c1].astype(F32) + tr[2, :, c0:c1].astype(F32)
                        + tr[3, :, c0:c1].astype(F32)) * (1.0 / (2 * NX))
        c = rc(mo.at[:, pl.ds(c0, c1 - c0)], mr.at[:, pl.ds(c0, c1 - c0)], hsend.at[u], hrecv.at[u], sib)
        c.start()
        hs.append(c)
        s_ref[half, c0:c1] = sp[half, c0:c1] - mo[:, c0:c1]

    def sketch_rest(u):
        c0, c1 = SUBS[u]
        hs[u].wait_recv()
        s_ref[rest, c0:c1] = sp[rest, c0:c1] - mr[at((2 * hm - ch) * (1 - core), ch - hm, 16), c0:c1]

    starts = [sum(K - i * NB for i in range(j)) for j in range(nb)]

    def gram(j, i0, i1):
        gp[starts[j] + (i0 - j) * NB:starts[j] + (i1 - j) * NB, :] = lax.dot_general(
            s_ref[:, i0 * NB:i1 * NB], s_ref[:, j * NB:(j + 1) * NB], (((0,), (0,)), ((), ())),
            precision=HI, preferred_element_type=F32)

    def copies(phase, g):
        a, n = GROUPS[g]
        q, m = n // NY, n // NY // NZ
        if phase == 1:
            return [rc(gp.at[at(a + q * lax.rem(y + d, NY), q, 8), :], yrv[g].at[d], ys1.at[g, d], yr1.at[g, d], ydev(d))
                    for d in YD]
        if phase == 2:
            return [rc(ybv[g].at[at(m * lax.rem(z + d, NZ), m, 8), :], zrv[g].at[d], zs1.at[g, d], zr1.at[g, d], zdev(d))
                    for d in ZD]
        if phase == 3:
            here = at(m * z, m, 8)
            return [rc(qfv[g].at[here, :], qfv[g].at[here, :], zs2.at[g, d], zr2.at[g, d], zdev(d)) for d in ZD]
        here = at(a + q * y, q, 8)
        return [rc(qfv[g], gr.at[here, :], ys2.at[g, d], yr2.at[g, d], ydev(d)) for d in YD]

    def send(phase, g):
        for c in copies(phase, g):
            c.start()

    def receive(phase, g):
        for c in copies(phase, g):
            c.wait_recv()

    def phase2(g):
        a, n = GROUPS[g]
        q = n // NY
        receive(1, g)
        ybv[g][...] = gp[at(a + q * y, q, 8), :] + yrv[g][1] + yrv[g][2] + yrv[g][3]
        send(2, g)

    def phase3(g):
        m = GROUPS[g][1] // NY // NZ
        receive(2, g)
        here = at(m * z, m, 8)
        tot = ybv[g][here, :]
        for d in range(1, NZ):
            tot = tot + zrv[g][d]
        qfv[g][here, :] = tot * (1.0 / D)
        send(3, g)

    def phase4(g):
        a, n = GROUPS[g]
        q = n // NY
        receive(3, g)
        send(4, g)
        gr[at(a + q * y, q, 8), :] = qfv[g][...]

    def basis_copy(j, d):
        cols = at(j * NB, NB, NB)
        return rc(bc.at[z, :, cols], bc.at[z, :, cols], bs.at[j, d], br.at[j, d], zdev(d))

    def send_column(j, ref, r0):
        cols = at(j * NB, NB, NB)
        bc[z, :, cols] = ref[r0:r0 + ch, cols].astype(BF16)
        for d in ZD:
            basis_copy(j, d).start()

    sketch_rest(0)
    gram(0, 0, 2)
    send(1, 0)
    send_column(0, s_ref, 0)
    sketch_rest(1)
    gram(0, 2, nb)
    gram(1, 1, nb)
    send(1, 1)
    gram(2, 2, nb)
    send(1, 2)
    gram(3, 3, nb)
    gram(4, 4, nb)
    gp[starts[4] + NB:, :] = jnp.zeros((STACK - starts[4] - NB, NB), F32)
    send(1, 3)
    phase2(0)
    f1.wait_recv()
    step = 64

    def pair(i, _):
        o = at(i * step, step, step)
        fb[o, :] = (wv[at(hf * core + i * step, step, step), :].astype(F32) + fw[o, :].astype(F32)).astype(BF16)
        return 0
    lax.fori_loop(0, hf // step, pair, 0)
    qx = hf // NX
    f2 = [rc(fb.at[at(qx * lax.rem(x + d, NX), qx, qx), :], fr.at[d], f2s.at[d], f2r.at[d], xdev(d)) for d in YD]
    for c in f2:
        c.start()
    phase2(1)
    phase2(2)
    phase3(0)
    phase2(3)
    phase3(1)
    x_ref[0:K, :] = jnp.zeros((K, K), F32)
    x_ref[K:K + ch, :] = s_ref[...]
    l_ref[...] = jnp.zeros((K, K), F32)
    out_ref[...] = jnp.zeros(out_ref.shape, F32)
    phase4(0)
    phase3(2)
    send_column(1, s_ref, 0)
    phase4(1)
    for c in f2:
        c.wait_recv()

    def four(i, _):
        o = at(i * 32, 32, 32)
        mw[at(hf * core + qx * x + i * 32, 32, 32), :] = (
            fb[at(qx * x + i * 32, 32, 32), :].astype(F32) + fr[1, o, :].astype(F32) + fr[2, o, :].astype(F32)
            + fr[3, o, :].astype(F32)).astype(BF16)
        return 0
    lax.fori_loop(0, qx // 32, four, 0)
    part = at(hf * core + qx * x, qx, qx)
    f3 = [rc(mw.at[part, :], mw.at[part, :], f3s.at[d], f3r.at[d], xdev(d)) for d in YD]
    for c in f3:
        c.start()
    phase3(3)
    send_column(2, s_ref, 0)
    receive(4, 0)
    x_ref[0:2 * NB, 0:NB] = gr[0:2 * NB, :]

    halfrows = at(hf * core, hf, hf)
    f4 = rc(mw.at[halfrows, :], mw.at[halfrows, :], f4s.at[0], f4r.at[0], sib)
    ysrc = z // 2

    def part_copy(j, d):
        cols = at(j * NB, NB, NB)
        return rc(ysb.at[d, :, cols], yrb.at[d, :, cols], ps.at[j, d], pr.at[j, d], ydev(d))

    def orth_copy(j, d):
        cols = at(j * NB, NB, NB)
        t = 4 * lax.rem(z, 2) + lax.rem(y + d, NY)
        return rc(bn.at[at(t * ch, ch, 16), cols], ob.at[:, cols], os_.at[j, d], or_.at[j], ydev(d))

    def factor(j):
        cols = at(j * NB, NB, NB)
        n_ref = ln_ref.at[j]
        t_ref[...] = x_ref[cols, cols]
        base_inverse(t_ref, n_ref)

        @pl.when(j == 0)
        def _():
            phase4(2)
            receive(4, 1)
            x_ref[2 * NB:K, 0:NB] = gr[2 * NB:K, :]
        p = lax.dot_general(x_ref[:, cols], n_ref[...], (((1,), (1,)), ((), ())), precision=HI,
                            preferred_element_type=F32)
        r = lax.broadcasted_iota(jnp.int32, (K, NB), 0)
        l_ref[:, cols] = jnp.where(r >= (j + 1) * NB, p[0:K], 0.0)

        @pl.when(j < nb - 1)
        def _():
            x_ref[...] = x_ref[...] - lax.dot_general(p, l_ref[:, cols], (((1,), (1,)), ((), ())), precision=HI,
                                                      preferred_element_type=F32)

        @pl.when(j < nb - AHEAD)
        def _():
            send_column(j + AHEAD, x_ref, K)

    def project(j):
        cols = at(j * NB, NB, NB)
        for d in ZD:
            basis_copy(j, d).wait_recv()
        for t in range(NZ):
            bn[t * NB:(t + 1) * NB, cols] = bc[t, 0:NB, cols]
            bn[NZ * NB + t * ex:NZ * NB + (t + 1) * ex, cols] = bc[t, NB:ch, cols]
        for d in (2, 1, 3):
            ysb[d, :, cols] = jnp.dot(dz[at(lax.rem(y + d, NY) * rows, rows, rows), :], bn[:, cols],
                                      preferred_element_type=F32).astype(BF16)
            part_copy(j, d).start()

        @pl.when(y == ysrc)
        def _():
            for d in YD:
                orth_copy(j, d).start()
            t = 4 * lax.rem(z, 2) + y
            ob[:, cols] = bn[at(t * ch, ch, 16), cols]
        out_ref[ch:, cols] = jnp.dot(dz[mine, :], bn[:, cols], preferred_element_type=F32)

    def finish(j):
        cols = at(j * NB, NB, NB)
        for d in YD:
            part_copy(j, d).wait_recv()

        @pl.when(y != ysrc)
        def _():
            orth_copy(j, 1).wait_recv()
        q = out_ref[ch:, cols] + (yrb[1, :, cols].astype(F32) + yrb[2, :, cols].astype(F32) + yrb[3, :, cols].astype(F32))
        col = lax.broadcasted_iota(jnp.int32, (NB, K), 1)
        first = jnp.maximum(j - AHEAD + 1, 0) * NB
        lrow = jnp.where((col >= first) & (col < j * NB), l_ref[cols, :], 0.0)
        prior = jnp.where(lax.broadcasted_iota(jnp.int32, out_ref.shape, 1) < j * NB, out_ref[...], 0.0)
        both = jnp.concatenate([ob[:, cols].astype(F32), q], axis=0) - lax.dot_general(
            prior, lrow, (((1,), (1,)), ((), ())), precision=HI, preferred_element_type=F32)
        out_ref[:, cols] = lax.dot_general(both, ln_ref[j], (((1,), (1,)), ((), ())), precision=HI,
                                           preferred_element_type=F32)

    def column(j, _):
        @pl.when(j == 1)
        def _():
            phase4(3)
            for c in f3:
                c.wait_recv()
            f4.start()
            receive(4, 2)
            n = K - NB
            x_ref[NB:K, NB:2 * NB] += gr[starts[1]:starts[1] + n, :]
            x_ref[2 * NB:3 * NB, 2 * NB:3 * NB] += gr[starts[2]:starts[2] + NB, :]
            f4.wait_recv()

            def delta(i, _):
                o = at(i * step, step, step)
                dz[o, :] = (wv[o, :].astype(F32) - mw[o, :].astype(F32) * (1.0 / (2 * NX))).astype(BF16)
                return 0
            lax.fori_loop(0, rr // step, delta, 0)
            project(0)

        @pl.when(j == 2)
        def _():
            receive(4, 3)
            x_ref[3 * NB:K, 2 * NB:3 * NB] += gr[starts[2] + NB:starts[3], :]
            x_ref[3 * NB:K, 3 * NB:4 * NB] += gr[starts[3]:starts[4], :]
            x_ref[4 * NB:K, 4 * NB:5 * NB] += gr[starts[4]:starts[4] + NB, :]
            project(1)

        @pl.when(j >= 2)
        def _():
            project(j)
        factor(j)

        @pl.when(j == 1)
        def _():
            finish(0)

        @pl.when(j == 2)
        def _():
            finish(1)

        @pl.when(j >= 2)
        def _():
            finish(j)
        return 0
    lax.fori_loop(0, nb, column, 0)

    done += gcs + gxs + fcs + [c for now in wcs + xs for c in now] + pairs + hs + [f1, f4] + f2 + f3
    for c in done + [c for phase in (1, 2, 3, 4) for g in range(len(GROUPS)) for c in copies(phase, g)]:
        c.wait_send()

    def drain(j, _):
        for d in ZD:
            basis_copy(j, d).wait_send()
        for d in YD:
            part_copy(j, d).wait_send()

        @pl.when(y == ysrc)
        def _():
            for d in YD:
                orth_copy(j, d).wait_send()
        return 0
    lax.fori_loop(0, nb, drain, 0)


def compress(w, g):
    rows, D = w.shape
    K = g.shape[1]
    cw = D // NY
    ch = cw // NZ
    rr = rows * NY
    nb = K // NB
    nu = len(SUBS)
    ng = len(GROUPS)
    V = pl.BlockSpec(memory_space=pltpu.VMEM)
    A = pl.BlockSpec(memory_space=pl.ANY)
    DM = pltpu.SemaphoreType.DMA
    M = pltpu.VMEM
    quarter = [n // NY for _, n in GROUPS]
    return pl.pallas_call(
        body,
        out_shape=jax.ShapeDtypeStruct((ch + rows, K), F32),
        in_specs=[A, A], out_specs=V,
        scratch_shapes=[
            M((rr, cw), BF16), M((rr, K), BF16), M((cw, K), F32), M((2, 4, ch, K), BF16), M((2, 4, ch, K), BF16),
            M((ch, K), F32), M((ch, K), F32), M((80, K), BF16), M((4, 80, K), BF16), M((80, K), F32), M((80, K), F32),
            M((ch, K), F32),
            M((STACK, NB), F32), M((STACK, NB), F32), [M((NY, q, NB), F32) for q in quarter], [M((q, NB), F32) for q in quarter],
            [M((NZ, q // NZ, NB), F32) for q in quarter], [M((q, NB), F32) for q in quarter],
            M((rr // 2, cw), BF16), M((rr // 2, cw), BF16), M((NX, rr // 2 // NX, cw), BF16), M((rr, cw), BF16), M((rr, cw), BF16),
            M((K + ch, K), F32), M((K, K), F32), M((nb, NB, NB), F32), M((NB, NB), F32),
            M((NZ, ch, K), BF16), M((cw, K), BF16), M((NY, rows, K), BF16), M((NY, rows, K), BF16), M((ch, K), BF16),
            DM((9, 4)), DM((9, 4)), DM((4,)), DM((4,)), DM((4, 4)), DM((4, 4)), DM((4,)), DM((4,)),
            DM((2, 4, nu)), DM((2, 4, nu)), DM((nu,)), DM((nu,)), DM((nu, 4)), DM((nu, 4)), DM((nu,)), DM((nu,)),
            DM((10,)), DM((1,)), DM((1,)), DM((4,)), DM((4,)), DM((4,)), DM((4,)), DM((1,)), DM((1,)),
            DM((ng, 4)), DM((ng, 4)), DM((ng, 8)), DM((ng, 8)), DM((ng, 8)), DM((ng, 8)), DM((ng, 4)), DM((ng, 4)),
            DM((nb, 8)), DM((nb, 8)), DM((nb, 4)), DM((nb, 4)), DM((nb, 4)), DM((nb,))],
        compiler_params=pltpu.CompilerParams(collective_id=0, has_side_effects=True, vmem_limit_bytes=60 * 2**20),
        name="delta_compress",
    )(w, g)


def on_device(weights, gaussian):
    both = compress(weights[0], gaussian)
    ch = both.shape[0] - weights.shape[1]
    return (both[None, :ch], both[None, ch:])


def solution(mesh):
    in_specs = (P("expert", "fsdp", None), P("fsdp", None))
    out_specs = (P("expert", "fsdp", None), P("expert", "fsdp", None))
    return jax.shard_map(
        on_device, mesh=mesh, in_specs=in_specs, out_specs=out_specs, check_vma=False
    )
```

time: 782 us -> 143 us (0.18)
  the two profiles are of different devices: /device:TPU:8 before, /device:TPU:1 now
where the time goes in v3:
time: 143 us
  Pallas kernels  138 us (97%)
  local copies, waits for them, and re-layouts  3.71 us (3%)
    pallas_call x1, Pallas kernels, compress(): pl.pallas_call(body, out_shape=jax.ShapeDtypeStruct((ch + rows, K), F32),...  138 us
    broadcast_in_dim x2, local copies, waits for them, and re-layouts, on_device(): return (both[None, :ch], both[None, ch:])  3.71 us

profile of v3, /device:TPU:1, one launch (start us, length us, event | category | flops | bytes accessed | tf_op | source)
XLA Modules:
  0.0 142.8 jit_solution(11490040997564830249)
XLA Ops:
  0.6 138.4 %delta_compress.1 = f32[400,640]{1,0:T(8,128)} custom-call(bf16[256,4608]{1,0:T(8,128)(2,1)} %bitcast.5, bf16[256,640]{1,0:T(8,128)(2,1)} %g_ref.1), custom_call_target="tpu_custom_call" | custom-call | tf_op jit(solution)/shard_map/delta_compress/pallas_call | solution.py:507
  139.1 1.7 %slice_bitcast_fusion.1 = f32[1,144,640]{2,1,0:T(8,128)} fusion(f32[400,640]{1,0:T(8,128)} %delta_compress.1), kind=kLoop, calls=%fused_computation.1 | loop fusion | bytes 737280 | tf_op jit(solution)/shard_map/broadcast_in_dim | solution.py:533
  140.8 2.0 %slice_bitcast_fusion = f32[1,256,640]{2,1,0:T(8,128)} fusion(f32[400,640]{1,0:T(8,128)} %delta_compress.1), kind=kLoop, calls=%fused_computation | loop fusion | bytes 1310720 | tf_op jit(solution)/shard_map/broadcast_in_dim | solution.py:533

commit v4 on v3

--- a/solution.py
+++ b/solution.py
@@ -14,6 +14,7 @@
 GROUPS = ((0, 256), (256, 512), (768, 512), (1280, 768))
 STACK = 2048
 AHEAD = 3
+PW = 64
 YD = (1, 3, 2)
 ZD = (1, 7, 2, 6, 3, 5, 4)
 
@@ -25,6 +26,10 @@
 
 def at(start, size, unit):
     return pl.ds(pl.multiple_of(start, unit), size)
+
+
+def wide(v):
+    return jnp.broadcast_to(v, (8, NB))
 
 
 def base_inverse(t_ref, n_ref):
@@ -32,42 +37,62 @@
     row = lax.broadcasted_iota(jnp.int32, (NB, NB), 0)
     col = lax.broadcasted_iota(jnp.int32, (NB, NB), 1)
     n_ref[...] = jnp.where(row == col, 1.0, 0.0).astype(F32)
-    nsub = NB // 8
-    wide = lambda v: jnp.broadcast_to(v, (8, NB))
-    cur_t, cur_n = t_ref[0:8, :], n_ref[0:8, :]
-    for b in range(nsub):
-        r0 = 8 * b
-        last = b == nsub - 1
-        c = [wide(cur_t[:, r0 + i:r0 + i + 1]) for i in range(8)]
-        if not last:
-            nt, nn = t_ref[r0 + 8:r0 + 16, :], n_ref[r0 + 8:r0 + 16, :]
-            d = [wide(nt[:, r0 + i:r0 + i + 1]) for i in range(8)]
-        for i in range(8):
-            rs = lax.rsqrt(wide(c[i][i:i + 1, :]))
-            m = c[i] * rs
-            mk = {}
-            for k in range(i + 1, 8):
-                mk[k] = wide(m[k:k + 1, :])
-                c[k] = c[k] - m * mk[k]
-            mm = jnp.where(sub > i, m, 0.0)
-            ft = wide(cur_t[i:i + 1, :]) * rs
-            fn = wide(cur_n[i:i + 1, :]) * rs
-            cur_t = jnp.where(sub == i, ft, cur_t - mm * ft)
-            cur_n = jnp.where(sub == i, fn, cur_n - mm * fn)
-            if not last:
-                md = d[i] * rs
+    npan = PW // 8
+    for p0 in range(0, NB, PW):
+        rt_ = [t_ref[p0 + 8 * s:p0 + 8 * s + 8, :] for s in range(npan)]
+        rn_ = [n_ref[p0 + 8 * s:p0 + 8 * s + 8, :] for s in range(npan)]
+        c = [wide(rt_[0][:, p0 + i:p0 + i + 1]) for i in range(8)]
+        for b in range(npan):
+            r0 = p0 + 8 * b
+            a = {(k, i): wide(c[i][k:k + 1, :]) for i in range(8) for k in range(i, 8)}
+            later = range(b + 1, npan)
+            dd = {s: [wide(rt_[s][:, r0 + i:r0 + i + 1]) for i in range(8)] for s in later}
+            if b + 1 < npan:
+                e = [wide(rt_[b + 1][:, r0 + 8 + i:r0 + 9 + i]) for i in range(8)]
+            l = {}
+            rs = []
+            for i in range(8):
+                r = lax.rsqrt(a[i, i])
+                rs.append(r)
                 for k in range(i + 1, 8):
-                    d[k] = d[k] - md * mk[k]
-                nt = nt - md * ft
-                nn = nn - md * fn
-        n_ref[r0:r0 + 8, :] = cur_n
-        if not last:
-            if b < nsub - 2:
-                both = jnp.concatenate([cur_t, cur_n], axis=1)
-                upd = lax.dot_general(cur_t, both, (((0,), (0,)), ((), ())), precision=HI, preferred_element_type=F32)
-                t_ref[r0 + 16:, :] = t_ref[r0 + 16:, :] - upd[r0 + 16:, :NB]
-                n_ref[r0 + 16:, :] = n_ref[r0 + 16:, :] - upd[r0 + 16:, NB:]
-            cur_t, cur_n = nt, nn
+                    l[k, i] = a[k, i] * r
+                for k in range(i + 1, 8):
+                    for k2 in range(k, 8):
+                        a[k2, k] = a[k2, k] - l[k2, i] * l[k, i]
+            rt = [wide(rt_[b][i:i + 1, :]) for i in range(8)]
+            rn = [wide(rn_[b][i:i + 1, :]) for i in range(8)]
+            for i in range(8):
+                rt[i] = rt[i] * rs[i]
+                rn[i] = rn[i] * rs[i]
+                for k in range(i + 1, 8):
+                    rt[k] = rt[k] - l[k, i] * rt[i]
+                    rn[k] = rn[k] - l[k, i] * rn[i]
+            for s in later:
+                d = dd[s]
+                for i in range(8):
+                    v = d[i] * rs[i]
+                    for k in range(i + 1, 8):
+                        d[k] = d[k] - v * l[k, i]
+                    rt_[s] = rt_[s] - v * rt[i]
+                    rn_[s] = rn_[s] - v * rn[i]
+                    if s == b + 1:
+                        for k in range(8):
+                            e[k] = e[k] - v * wide(v[k:k + 1, :])
+            ct, cn = rt[0], rn[0]
+            for i in range(1, 8):
+                ct = jnp.where(sub == i, rt[i], ct)
+                cn = jnp.where(sub == i, rn[i], cn)
+            rt_[b], rn_[b] = ct, cn
+            n_ref[r0:r0 + 8, :] = cn
+            if b + 1 < npan:
+                c = e
+        q0 = p0 + PW
+        if q0 < NB:
+            lt = jnp.concatenate(rt_, axis=0)
+            both = jnp.concatenate([lt, jnp.concatenate(rn_, axis=0)], axis=1)
+            upd = lax.dot_general(lt, both, (((0,), (0,)), ((), ())), precision=HI, preferred_element_type=F32)
+            t_ref[q0:, :] = t_ref[q0:, :] - upd[q0:, :NB]
+            n_ref[q0:, :] = n_ref[q0:, :] - upd[q0:, NB:]
 
 
 def body(w_ref, g_ref, out_ref,
@@ -185,6 +210,9 @@
                 done.append(c)
                 prev[dr, u] = c
     product(8)
+    hf = rr // 2
+    f1 = rc(wv.at[at(hf * (1 - core), hf, hf), :], fw, f1s.at[0], f1r.at[0], sib)
+    f1.start()
     hm = 80
     half = at((ch - hm) * core, hm, 16)
     rest = at(hm * (1 - core), ch - hm, 16)
@@ -196,8 +224,6 @@
         c = rc(sp.at[:, pl.ds(c0, c1 - c0)], sx.at[:, pl.ds(c0, c1 - c0)], csend.at[u], crecv.at[u], sib)
         c.start()
         pairs.append(c)
-    hf = rr // 2
-    f1 = rc(wv.at[at(hf * (1 - core), hf, hf), :], fw, f1s.at[0], f1r.at[0], sib)
     xs = []
     for u, (c0, c1) in enumerate(SUBS):
         pairs[u].wait_recv()
@@ -209,7 +235,18 @@
             c.start()
             now.append(c)
         xs.append(now)
-    f1.start()
+    f1.wait_recv()
+    step = 64
+
+    def pair(i, _):
+        o = at(i * step, step, step)
+        fb[o, :] = (wv[at(hf * core + i * step, step, step), :].astype(F32) + fw[o, :].astype(F32)).astype(BF16)
+        return 0
+    lax.fori_loop(0, hf // step, pair, 0)
+    qx = hf // NX
+    f2 = [rc(fb.at[at(qx * lax.rem(x + d, NX), qx, qx), :], fr.at[d], f2s.at[d], f2r.at[d], xdev(d)) for d in YD]
+    for c in f2:
+        c.start()
     hs = []
     for u, (c0, c1) in enumerate(SUBS):
         for c in xs[u]:
@@ -305,19 +342,21 @@
     gp[starts[4] + NB:, :] = jnp.zeros((STACK - starts[4] - NB, NB), F32)
     send(1, 3)
     phase2(0)
-    f1.wait_recv()
-    step = 64
-
-    def pair(i, _):
-        o = at(i * step, step, step)
-        fb[o, :] = (wv[at(hf * core + i * step, step, step), :].astype(F32) + fw[o, :].astype(F32)).astype(BF16)
+    phase2(1)
+    for c in f2:
+        c.wait_recv()
+
+    def four(i, _):
+        o = at(i * 32, 32, 32)
+        mw[at(hf * core + qx * x + i * 32, 32, 32), :] = (
+            fb[at(qx * x + i * 32, 32, 32), :].astype(F32) + fr[1, o, :].astype(F32) + fr[2, o, :].astype(F32)
+            + fr[3, o, :].astype(F32)).astype(BF16)
         return 0
-    lax.fori_loop(0, hf // step, pair, 0)
-    qx = hf // NX
-    f2 = [rc(fb.at[at(qx * lax.rem(x + d, NX), qx, qx), :], fr.at[d], f2s.at[d], f2r.at[d], xdev(d)) for d in YD]
-    for c in f2:
+    lax.fori_loop(0, qx // 32, four, 0)
+    part = at(hf * core + qx * x, qx, qx)
+    f3 = [rc(mw.at[part, :], mw.at[part, :], f3s.at[d], f3r.at[d], xdev(d)) for d in YD]
+    for c in f3:
         c.start()
-    phase2(1)
     phase2(2)
     phase3(0)
     phase2(3)
@@ -330,20 +369,6 @@
     phase3(2)
     send_column(1, s_ref, 0)
     phase4(1)
-    for c in f2:
-        c.wait_recv()
-
-    def four(i, _):
-        o = at(i * 32, 32, 32)
-        mw[at(hf * core + qx * x + i * 32, 32, 32), :] = (
-            fb[at(qx * x + i * 32, 32, 32), :].astype(F32) + fr[1, o, :].astype(F32) + fr[2, o, :].astype(F32)
-            + fr[3, o, :].astype(F32)).astype(BF16)
-        return 0
-    lax.fori_loop(0, qx // 32, four, 0)
-    part = at(hf * core + qx * x, qx, qx)
-    f3 = [rc(mw.at[part, :], mw.at[part, :], f3s.at[d], f3r.at[d], xdev(d)) for d in YD]
-    for c in f3:
-        c.start()
     phase3(3)
     send_column(2, s_ref, 0)
     receive(4, 0)
@@ -371,6 +396,16 @@
         @pl.when(j == 0)
         def _():
             phase4(2)
+            for c in f3:
+                c.wait_recv()
+            f4.start()
+            f4.wait_recv()
+
+            def delta(i, _):
+                o = at(i * step, step, step)
+                dz[o, :] = (wv[o, :].astype(F32) - mw[o, :].astype(F32) * (1.0 / (2 * NX))).astype(BF16)
+                return 0
+            lax.fori_loop(0, rr // step, delta, 0)
             receive(4, 1)
             x_ref[2 * NB:K, 0:NB] = gr[2 * NB:K, :]
         p = lax.dot_general(x_ref[:, cols], n_ref[...], (((1,), (1,)), ((), ())), precision=HI,
@@ -378,10 +413,12 @@
         r = lax.broadcasted_iota(jnp.int32, (K, NB), 0)
         l_ref[:, cols] = jnp.where(r >= (j + 1) * NB, p[0:K], 0.0)
 
-        @pl.when(j < nb - 1)
-        def _():
-            x_ref[...] = x_ref[...] - lax.dot_general(p, l_ref[:, cols], (((1,), (1,)), ((), ())), precision=HI,
-                                                      preferred_element_type=F32)
+        for k in range(nb - 1):
+            @pl.when(j == k)
+            def _(k=k):
+                o = (k + 1) * NB
+                x_ref[o:, o:] = x_ref[o:, o:] - lax.dot_general(p[o:], p[o:K], (((1,), (1,)), ((), ())), precision=HI,
+                                                                preferred_element_type=F32)
 
         @pl.when(j < nb - AHEAD)
         def _():
@@ -416,10 +453,11 @@
         def _():
             orth_copy(j, 1).wait_recv()
         q = out_ref[ch:, cols] + (yrb[1, :, cols].astype(F32) + yrb[2, :, cols].astype(F32) + yrb[3, :, cols].astype(F32))
-        col = lax.broadcasted_iota(jnp.int32, (NB, K), 1)
         first = jnp.maximum(j - AHEAD + 1, 0) * NB
-        lrow = jnp.where((col >= first) & (col < j * NB), l_ref[cols, :], 0.0)
-        prior = jnp.where(lax.broadcasted_iota(jnp.int32, out_ref.shape, 1) < j * NB, out_ref[...], 0.0)
+        seen = at(first, (AHEAD - 1) * NB, NB)
+        col = lax.broadcasted_iota(jnp.int32, (NB, (AHEAD - 1) * NB), 1)
+        lrow = jnp.where(col + first < j * NB, l_ref[cols, seen], 0.0)
+        prior = out_ref[:, seen]
         both = jnp.concatenate([ob[:, cols].astype(F32), q], axis=0) - lax.dot_general(
             prior, lrow, (((1,), (1,)), ((), ())), precision=HI, preferred_element_type=F32)
         out_ref[:, cols] = lax.dot_general(both, ln_ref[j], (((1,), (1,)), ((), ())), precision=HI,
@@ -429,20 +467,10 @@
         @pl.when(j == 1)
         def _():
             phase4(3)
-            for c in f3:
-                c.wait_recv()
-            f4.start()
             receive(4, 2)
             n = K - NB
             x_ref[NB:K, NB:2 * NB] += gr[starts[1]:starts[1] + n, :]
             x_ref[2 * NB:3 * NB, 2 * NB:3 * NB] += gr[starts[2]:starts[2] + NB, :]
-            f4.wait_recv()
-
-            def delta(i, _):
-                o = at(i * step, step, step)
-                dz[o, :] = (wv[o, :].astype(F32) - mw[o, :].astype(F32) * (1.0 / (2 * NX))).astype(BF16)
-                return 0
-            lax.fori_loop(0, rr // step, delta, 0)
             project(0)
 
         @pl.when(j == 2)
@@ -527,10 +555,27 @@
     )(w, g)
 
 
+def split_body(both_ref, orth_ref, proj_ref):
+    ch = orth_ref.shape[0]
+    orth_ref[...] = both_ref[:ch, :]
+    proj_ref[...] = both_ref[ch:, :]
+
+
+def split(both, ch):
+    n, K = both.shape
+    V = pl.BlockSpec(memory_space=pltpu.VMEM)
+    return pl.pallas_call(
+        split_body,
+        out_shape=(jax.ShapeDtypeStruct((ch, K), F32), jax.ShapeDtypeStruct((n - ch, K), F32)),
+        in_specs=[V], out_specs=(V, V),
+        name="split_outputs",
+    )(both)
+
+
 def on_device(weights, gaussian):
     both = compress(weights[0], gaussian)
-    ch = both.shape[0] - weights.shape[1]
-    return (both[None, :ch], both[None, ch:])
+    orthonormal, projection = split(both, both.shape[0] - weights.shape[1])
+    return (orthonormal[None], projection[None])
 
 
 def solution(mesh):

time: 143 us -> 126 us (0.88)
  the two profiles are of different devices: /device:TPU:1 before, /device:TPU:8 now
where the time goes in v4:
time: 126 us; the launch traced here: 124 us
  Pallas kernels  124 us (98%)
    pallas_call x1, Pallas kernels, compress(): pl.pallas_call(body, out_shape=jax.ShapeDtypeStruct((ch + rows, K), F32),...  122 us

profile of v4, /device:TPU:8, one launch (start us, length us, event | category | flops | bytes accessed | tf_op | source)
XLA Modules:
  0.0 124.4 jit_solution(3343366937830972073)
XLA Ops:
  0.6 121.5 %delta_compress.1.both_ref = f32[400,640]{1,0:T(8,128)} custom-call(bf16[256,4608]{1,0:T(8,128)(2,1)} %bitcast.3, bf16[256,640]{1,0:T(8,128)(2,1)} %g_ref.1), custom_call_target="tpu_custom_call" | custom-call | tf_op jit(solution)/shard_map/delta_compress/pallas_call | solution.py:535
  122.2 2.2 %split_outputs.1 = (f32[144,640]{1,0:T(8,128)}, f32[256,640]{1,0:T(8,128)}) custom-call(f32[400,640]{1,0:T(8,128)} %delta_compress.1.both_ref), custom_call_target="tpu_custom_call" | custom-call | tf_op jit(solution)/shard_map/split_outputs/pallas_call | solution.py:567

commit v5 on v4

--- a/solution.py
+++ b/solution.py
@@ -13,7 +13,6 @@
 SUBS = ((0, 256), (256, 640))
 GROUPS = ((0, 256), (256, 512), (768, 512), (1280, 768))
 STACK = 2048
-AHEAD = 3
 PW = 64
 YD = (1, 3, 2)
 ZD = (1, 7, 2, 6, 3, 5, 4)
@@ -98,7 +97,7 @@
 def body(w_ref, g_ref, out_ref,
          wv, gv, p_ref, sbuf, rbuf, sp, sx, tb, tr, mo, mr, s_ref,
          gp, gr, yrv, ybv, zrv, qfv,
-         fw, fb, fr, mw, dz, x_ref, l_ref, ln_ref, t_ref, bc, bn, ysb, yrb, ob,
+         fw, fb, fr, mw, dz, x_ref, l_ref, ln_ref, t_ref, bn, ysb, yrb, ob,
          wsend, wrecv, gsend, grecv, gxsend, gxrecv, fsend, frecv, zsend, zrecv, csend, crecv, xsend, xrecv, hsend, hrecv,
          loc, f1s, f1r, f2s, f2r, f3s, f3r, f4s, f4r, ys1, yr1, zs1, zr1, zs2, zr2, ys2, yr2, bs, br, ps, pr, os_, or_):
     rows, D = w_ref.shape
@@ -317,21 +316,30 @@
         send(4, g)
         gr[at(a + q * y, q, 8), :] = qfv[g][...]
 
-    def basis_copy(j, d):
-        cols = at(j * NB, NB, NB)
-        return rc(bc.at[z, :, cols], bc.at[z, :, cols], bs.at[j, d], br.at[j, d], zdev(d))
-
-    def send_column(j, ref, r0):
-        cols = at(j * NB, NB, NB)
-        bc[z, :, cols] = ref[r0:r0 + ch, cols].astype(BF16)
-        for d in ZD:
-            basis_copy(j, d).start()
+    def gather_copies(step, dr):
+        b = lax.rem(z + (NZ - step if dr == 0 else step), NZ)
+        r, n = (0, NB) if step < 3 else ((0, ha) if dr == 0 else (ha, NB - ha))
+        pieces = [at(b * NB + r, n, 16)]
+        if step < 3 or dr == 1:
+            pieces.append(at(NZ * NB + b * ex, ex, 16))
+        to = zdev(1 if dr == 0 else NZ - 1)
+        return [rc(bn.at[o, :], bn.at[o, :], bs.at[step, dr, i], br.at[step, dr, i], to) for i, o in enumerate(pieces)]
+
+    def gather(step):
+        for dr in (0, 1):
+            if step:
+                for c in gather_copies(step - 1, dr):
+                    c.wait_recv()
+            for c in gather_copies(step, dr):
+                c.start()
 
     sketch_rest(0)
     gram(0, 0, 2)
     send(1, 0)
-    send_column(0, s_ref, 0)
     sketch_rest(1)
+    bn[at(z * NB, NB, NB), :] = s_ref[0:NB, :].astype(BF16)
+    bn[at(NZ * NB + z * ex, ex, 16), :] = s_ref[NB:, :].astype(BF16)
+    gather(0)
     gram(0, 2, nb)
     gram(1, 1, nb)
     send(1, 1)
@@ -343,6 +351,7 @@
     send(1, 3)
     phase2(0)
     phase2(1)
+    gather(1)
     for c in f2:
         c.wait_recv()
 
@@ -361,16 +370,13 @@
     phase3(0)
     phase2(3)
     phase3(1)
+    gather(2)
     x_ref[0:K, :] = jnp.zeros((K, K), F32)
-    x_ref[K:K + ch, :] = s_ref[...]
-    l_ref[...] = jnp.zeros((K, K), F32)
-    out_ref[...] = jnp.zeros(out_ref.shape, F32)
     phase4(0)
     phase3(2)
-    send_column(1, s_ref, 0)
     phase4(1)
+    gather(3)
     phase3(3)
-    send_column(2, s_ref, 0)
     receive(4, 0)
     x_ref[0:2 * NB, 0:NB] = gr[0:2 * NB, :]
 
@@ -382,10 +388,46 @@
         cols = at(j * NB, NB, NB)
         return rc(ysb.at[d, :, cols], yrb.at[d, :, cols], ps.at[j, d], pr.at[j, d], ydev(d))
 
-    def orth_copy(j, d):
-        cols = at(j * NB, NB, NB)
+    def orth_copy(d):
         t = 4 * lax.rem(z, 2) + lax.rem(y + d, NY)
-        return rc(bn.at[at(t * ch, ch, 16), cols], ob.at[:, cols], os_.at[j, d], or_.at[j], ydev(d))
+        return rc(bn.at[at(t * ch, ch, 16), :], ob, os_.at[d], or_.at[0], ydev(d))
+
+    def place_rows():
+        for dr in (0, 1):
+            for c in gather_copies(3, dr):
+                c.wait_recv()
+
+        @pl.when(y == ysrc)
+        def _():
+            for d in YD:
+                orth_copy(d).start()
+            t = 4 * lax.rem(z, 2) + y
+            ob[...] = bn[at(t * ch, ch, 16), :]
+
+    def project():
+        for d in (2, 1, 3):
+            ysb[d] = jnp.dot(dz[at(lax.rem(y + d, NY) * rows, rows, rows), :], bn[...], preferred_element_type=F32).astype(BF16)
+            for j in range(nb):
+                part_copy(j, d).start()
+
+        out_ref[ch:, :] = jnp.dot(dz[mine, :], bn[...], preferred_element_type=F32)
+
+    def finish(k):
+        cols = slice(k * NB, (k + 1) * NB)
+        if k == 0:
+            @pl.when(y != ysrc)
+            def _():
+                orth_copy(1).wait_recv()
+            out_ref[:ch, :] = ob[...].astype(F32)
+        for d in YD:
+            part_copy(k, d).wait_recv()
+        out_ref[ch:, cols] += (yrb[1, :, cols].astype(F32) + yrb[2, :, cols].astype(F32) + yrb[3, :, cols].astype(F32))
+        out_ref[:, cols] = lax.dot_general(out_ref[:, cols], ln_ref[k], (((1,), (1,)), ((), ())), precision=HI,
+                                           preferred_element_type=F32)
+        if k < nb - 1:
+            after = (k + 1) * NB
+            out_ref[:, after:] -= lax.dot_general(out_ref[:, cols], l_ref[after:, cols], (((1,), (1,)), ((), ())),
+                                                  precision=HI, preferred_element_type=F32)
 
     def factor(j):
         cols = at(j * NB, NB, NB)
@@ -396,6 +438,7 @@
         @pl.when(j == 0)
         def _():
             phase4(2)
+            place_rows()
             for c in f3:
                 c.wait_recv()
             f4.start()
@@ -406,72 +449,27 @@
                 dz[o, :] = (wv[o, :].astype(F32) - mw[o, :].astype(F32) * (1.0 / (2 * NX))).astype(BF16)
                 return 0
             lax.fori_loop(0, rr // step, delta, 0)
+            phase4(3)
             receive(4, 1)
             x_ref[2 * NB:K, 0:NB] = gr[2 * NB:K, :]
-        p = lax.dot_general(x_ref[:, cols], n_ref[...], (((1,), (1,)), ((), ())), precision=HI,
-                            preferred_element_type=F32)
-        r = lax.broadcasted_iota(jnp.int32, (K, NB), 0)
-        l_ref[:, cols] = jnp.where(r >= (j + 1) * NB, p[0:K], 0.0)
-
         for k in range(nb - 1):
             @pl.when(j == k)
             def _(k=k):
-                o = (k + 1) * NB
-                x_ref[o:, o:] = x_ref[o:, o:] - lax.dot_general(p[o:], p[o:K], (((1,), (1,)), ((), ())), precision=HI,
+                a, b = k * NB, (k + 1) * NB
+                p = lax.dot_general(x_ref[b:, a:b], n_ref[...], (((1,), (1,)), ((), ())), precision=HI,
+                                    preferred_element_type=F32)
+                l_ref[b:, a:b] = p
+                x_ref[b:, b:] = x_ref[b:, b:] - lax.dot_general(p, p, (((1,), (1,)), ((), ())), precision=HI,
                                                                 preferred_element_type=F32)
-
-        @pl.when(j < nb - AHEAD)
-        def _():
-            send_column(j + AHEAD, x_ref, K)
-
-    def project(j):
-        cols = at(j * NB, NB, NB)
-        for d in ZD:
-            basis_copy(j, d).wait_recv()
-        for t in range(NZ):
-            bn[t * NB:(t + 1) * NB, cols] = bc[t, 0:NB, cols]
-            bn[NZ * NB + t * ex:NZ * NB + (t + 1) * ex, cols] = bc[t, NB:ch, cols]
-        for d in (2, 1, 3):
-            ysb[d, :, cols] = jnp.dot(dz[at(lax.rem(y + d, NY) * rows, rows, rows), :], bn[:, cols],
-                                      preferred_element_type=F32).astype(BF16)
-            part_copy(j, d).start()
-
-        @pl.when(y == ysrc)
-        def _():
-            for d in YD:
-                orth_copy(j, d).start()
-            t = 4 * lax.rem(z, 2) + y
-            ob[:, cols] = bn[at(t * ch, ch, 16), cols]
-        out_ref[ch:, cols] = jnp.dot(dz[mine, :], bn[:, cols], preferred_element_type=F32)
-
-    def finish(j):
-        cols = at(j * NB, NB, NB)
-        for d in YD:
-            part_copy(j, d).wait_recv()
-
-        @pl.when(y != ysrc)
-        def _():
-            orth_copy(j, 1).wait_recv()
-        q = out_ref[ch:, cols] + (yrb[1, :, cols].astype(F32) + yrb[2, :, cols].astype(F32) + yrb[3, :, cols].astype(F32))
-        first = jnp.maximum(j - AHEAD + 1, 0) * NB
-        seen = at(first, (AHEAD - 1) * NB, NB)
-        col = lax.broadcasted_iota(jnp.int32, (NB, (AHEAD - 1) * NB), 1)
-        lrow = jnp.where(col + first < j * NB, l_ref[cols, seen], 0.0)
-        prior = out_ref[:, seen]
-        both = jnp.concatenate([ob[:, cols].astype(F32), q], axis=0) - lax.dot_general(
-            prior, lrow, (((1,), (1,)), ((), ())), precision=HI, preferred_element_type=F32)
-        out_ref[:, cols] = lax.dot_general(both, ln_ref[j], (((1,), (1,)), ((), ())), precision=HI,
-                                           preferred_element_type=F32)
 
     def column(j, _):
         @pl.when(j == 1)
         def _():
-            phase4(3)
+            project()
             receive(4, 2)
             n = K - NB
             x_ref[NB:K, NB:2 * NB] += gr[starts[1]:starts[1] + n, :]
             x_ref[2 * NB:3 * NB, 2 * NB:3 * NB] += gr[starts[2]:starts[2] + NB, :]
-            project(0)
 
         @pl.when(j == 2)
         def _():
@@ -479,43 +477,33 @@
             x_ref[3 * NB:K, 2 * NB:3 * NB] += gr[starts[2] + NB:starts[3], :]
             x_ref[3 * NB:K, 3 * NB:4 * NB] += gr[starts[3]:starts[4], :]
             x_ref[4 * NB:K, 4 * NB:5 * NB] += gr[starts[4]:starts[4] + NB, :]
-            project(1)
-
-        @pl.when(j >= 2)
-        def _():
-            project(j)
+
         factor(j)
-
-        @pl.when(j == 1)
-        def _():
-            finish(0)
-
-        @pl.when(j == 2)
-        def _():
-            finish(1)
-
-        @pl.when(j >= 2)
-        def _():
-            finish(j)
+        for k in range(nb - 2):
+            @pl.when(j == k + 2)
+            def _(k=k):
+                finish(k)
         return 0
     lax.fori_loop(0, nb, column, 0)
+    finish(nb - 2)
+    finish(nb - 1)
 
     done += gcs + gxs + fcs + [c for now in wcs + xs for c in now] + pairs + hs + [f1, f4] + f2 + f3
     for c in done + [c for phase in (1, 2, 3, 4) for g in range(len(GROUPS)) for c in copies(phase, g)]:
         c.wait_send()
 
-    def drain(j, _):
-        for d in ZD:
-            basis_copy(j, d).wait_send()
+    for dr in (0, 1):
+        for step in range(4):
+            for c in gather_copies(step, dr):
+                c.wait_send()
+    for j in range(nb):
         for d in YD:
             part_copy(j, d).wait_send()
 
-        @pl.when(y == ysrc)
-        def _():
-            for d in YD:
-                orth_copy(j, d).wait_send()
-        return 0
-    lax.fori_loop(0, nb, drain, 0)
+    @pl.when(y == ysrc)
+    def _():
+        for d in YD:
+            orth_copy(d).wait_send()
 
 
 def compress(w, g):
@@ -543,13 +531,13 @@
             M((STACK, NB), F32), M((STACK, NB), F32), [M((NY, q, NB), F32) for q in quarter], [M((q, NB), F32) for q in quarter],
             [M((NZ, q // NZ, NB), F32) for q in quarter], [M((q, NB), F32) for q in quarter],
             M((rr // 2, cw), BF16), M((rr // 2, cw), BF16), M((NX, rr // 2 // NX, cw), BF16), M((rr, cw), BF16), M((rr, cw), BF16),
-            M((K + ch, K), F32), M((K, K), F32), M((nb, NB, NB), F32), M((NB, NB), F32),
-            M((NZ, ch, K), BF16), M((cw, K), BF16), M((NY, rows, K), BF16), M((NY, rows, K), BF16), M((ch, K), BF16),
+            M((K, K), F32), M((K, K), F32), M((nb, NB, NB), F32), M((NB, NB), F32),
+            M((cw, K), BF16), M((NY, rows, K), BF16), M((NY, rows, K), BF16), M((ch, K), BF16),
             DM((9, 4)), DM((9, 4)), DM((4,)), DM((4,)), DM((4, 4)), DM((4, 4)), DM((4,)), DM((4,)),
             DM((2, 4, nu)), DM((2, 4, nu)), DM((nu,)), DM((nu,)), DM((nu, 4)), DM((nu, 4)), DM((nu,)), DM((nu,)),
             DM((10,)), DM((1,)), DM((1,)), DM((4,)), DM((4,)), DM((4,)), DM((4,)), DM((1,)), DM((1,)),
             DM((ng, 4)), DM((ng, 4)), DM((ng, 8)), DM((ng, 8)), DM((ng, 8)), DM((ng, 8)), DM((ng, 4)), DM((ng, 4)),
-            DM((nb, 8)), DM((nb, 8)), DM((nb, 4)), DM((nb, 4)), DM((nb, 4)), DM((nb,))],
+            DM((4, 2, 2)), DM((4, 2, 2)), DM((nb, 4)), DM((nb, 4)), DM((4,)), DM((1,))],
         compiler_params=pltpu.CompilerParams(collective_id=0, has_side_effects=True, vmem_limit_bytes=60 * 2**20),
         name="delta_compress",
     )(w, g)

time: 126 us -> 123 us (0.976); the launches traced: 124 us -> 123 us
  Pallas kernels: 124 us -> 122 us
    pallas_call x1, Pallas kernels: 122 us -> 120 us  [compress(): pl.pallas_call(body, out_shape=jax.ShapeDtypeStruct((ch + rows, K), F32),...]
where the time goes in v5:
time: 123 us
  Pallas kernels  122 us (99%)
    pallas_call x1, Pallas kernels, compress(): pl.pallas_call(body, out_shape=jax.ShapeDtypeStruct((ch + rows, K), F32),...  120 us

profile of v5, /device:TPU:8, one launch (start us, length us, event | category | flops | bytes accessed | tf_op | source)
XLA Modules:
  0.0 122.9 jit_solution(10485068085902222275)
XLA Ops:
  0.6 120.1 %delta_compress.1.both_ref = f32[400,640]{1,0:T(8,128)} custom-call(bf16[256,4608]{1,0:T(8,128)(2,1)} %bitcast.3, bf16[256,640]{1,0:T(8,128)(2,1)} %g_ref.1), custom_call_target="tpu_custom_call" | custom-call | tf_op jit(solution)/shard_map/delta_compress/pallas_call | solution.py:523
  120.7 2.2 %split_outputs.1 = (f32[144,640]{1,0:T(8,128)}, f32[256,640]{1,0:T(8,128)}) custom-call(f32[400,640]{1,0:T(8,128)} %delta_compress.1.both_ref), custom_call_target="tpu_custom_call" | custom-call | tf_op jit(solution)/shard_map/split_outputs/pallas_call | solution.py:555

commit v6 on v5

--- a/solution.py
+++ b/solution.py
@@ -352,6 +352,8 @@
     phase2(0)
     phase2(1)
     gather(1)
+    phase2(2)
+    phase3(0)
     for c in f2:
         c.wait_recv()
 
@@ -366,8 +368,6 @@
     f3 = [rc(mw.at[part, :], mw.at[part, :], f3s.at[d], f3r.at[d], xdev(d)) for d in YD]
     for c in f3:
         c.start()
-    phase2(2)
-    phase3(0)
     phase2(3)
     phase3(1)
     gather(2)

time: 123 us -> 123 us (level)
  no operation moved by 1% of the time
where the time goes in v6:
time: 123 us
  Pallas kernels  122 us (99%)
    pallas_call x1, Pallas kernels, compress(): pl.pallas_call(body, out_shape=jax.ShapeDtypeStruct((ch + rows, K), F32),...  120 us

profile of v6, /device:TPU:8, one launch (start us, length us, event | category | flops | bytes accessed | tf_op | source)
XLA Modules:
  0.0 122.9 jit_solution(15179118506654626308)
XLA Ops:
  0.6 120.1 %delta_compress.1.both_ref = f32[400,640]{1,0:T(8,128)} custom-call(bf16[256,4608]{1,0:T(8,128)(2,1)} %bitcast.3, bf16[256,640]{1,0:T(8,128)(2,1)} %g_ref.1), custom_call_target="tpu_custom_call" | custom-call | tf_op jit(solution)/shard_map/delta_compress/pallas_call | solution.py:523
  120.7 2.2 %split_outputs.1 = (f32[144,640]{1,0:T(8,128)}, f32[256,640]{1,0:T(8,128)}) custom-call(f32[400,640]{1,0:T(8,128)} %delta_compress.1.both_ref), custom_call_target="tpu_custom_call" | custom-call | tf_op jit(solution)/shard_map/split_outputs/pallas_call | solution.py:555
